TPU v7x, 512 devices: a whole 4x4x16 slice. The times are simulated.
512 devices in a mesh: seq: 64 (over x, z), exp: 8 (over y, core).
Axes of the slice: x: 4, y: 4, z: 16, core: 2. Of those that a mesh axis runs over, the one named last changes fastest.
Arguments:
- tokens: bfloat16 [16384, 6144], P('seq', 'exp'), may hold values from -24 to 24
- slot_param: bfloat16 [256, 6144], P('exp', 'seq'), may hold values from -4 to 4
- slot_outputs: bfloat16 [256, 6144], P('exp', 'seq'), may hold values from -6 to 6
- grad_output: bfloat16 [16384, 6144], P('seq', 'exp'), may hold values from -6 to 6
- grad_slot_in: bfloat16 [256, 6144], P('exp', 'seq'), may hold values from -6 to 6
Outputs:
- slot_inputs: bfloat16 [256, 6144], P('exp', 'seq')
- layer_output: bfloat16 [16384, 6144], P('seq', 'exp')
- grad_tokens: bfloat16 [16384, 6144], P('seq', 'exp')
- grad_param: bfloat16 [256, 6144], P('exp', 'seq')
- grad_slot_out: bfloat16 [256, 6144], P('exp', 'seq')
All inputs are finite; a program needn't handle non-finite values.
Results may differ from a plain program's by a relative error of at most 0.0057.
Values may be sent and summed in bfloat16 or wider, within the bound.
A program may use at most 64 MiB of HBM per device.

v0:
```python
import jax
import jax.numpy as jnp
from jax import lax
from jax.sharding import PartitionSpec as P


def contract_last(left_arr, right_arr):
    return lax.dot_general(
        left_arr, right_arr, (((1,), (1,)), ((), ())), preferred_element_type=jnp.float32
    )


def contract_first(left_arr, right_arr):
    return lax.dot_general(
        left_arr, right_arr, (((0,), (0,)), ((), ())), preferred_element_type=jnp.float32
    )


def shards(tokens, slot_param, slot_outputs, grad_output, grad_slot_in):
    gathered = (
        lax.all_gather(slot_param, "seq", axis=1, tiled=True),
        lax.all_gather(slot_outputs, "seq", axis=1, tiled=True),
        lax.all_gather(grad_slot_in, "seq", axis=1, tiled=True),
    )
    param_cols, output_cols, cotan_cols = (
        lax.all_to_all(gathered[0], "exp", split_axis=1, concat_axis=0, tiled=True),
        lax.all_to_all(gathered[1], "exp", split_axis=1, concat_axis=0, tiled=True),
        lax.all_to_all(gathered[2], "exp", split_axis=1, concat_axis=0, tiled=True),
    )
    logits = lax.psum(contract_last(tokens, param_cols), "exp")
    col_max = lax.pmax(jnp.max(logits, axis=0), "seq")
    col_total = lax.psum(jnp.sum(jnp.exp(logits - col_max), axis=0), "seq")
    dispatch_full = jnp.exp(logits - col_max) / col_total
    dispatch = dispatch_full.astype(jnp.bfloat16)
    row_max = jnp.max(logits, axis=1, keepdims=True)
    row_weights = jnp.exp(logits - row_max)
    combine_full = row_weights / jnp.sum(row_weights, axis=1, keepdims=True)
    combine = combine_full.astype(jnp.bfloat16)
    slot_part = contract_first(dispatch, tokens)
    layer_output = jnp.dot(combine, output_cols, preferred_element_type=jnp.float32).astype(
        jnp.bfloat16
    )
    back_part = contract_first(combine, grad_output)
    grad_combine, grad_dispatch = lax.psum(
        (contract_last(grad_output, output_cols), contract_last(tokens, cotan_cols)), "exp"
    )
    from_combine = combine_full * (
        grad_combine - jnp.sum(combine_full * grad_combine, axis=1, keepdims=True)
    )
    column_sum = lax.psum(jnp.sum(dispatch_full * grad_dispatch, axis=0), "seq")
    from_dispatch = dispatch_full * (grad_dispatch - column_sum)
    grad_logits = (from_combine + from_dispatch).astype(jnp.bfloat16)
    grad_tokens = (
        jnp.dot(dispatch, cotan_cols, preferred_element_type=jnp.float32)
        + jnp.dot(grad_logits, param_cols, preferred_element_type=jnp.float32)
    ).astype(jnp.bfloat16)
    param_part = contract_first(grad_logits, tokens)
    partials = (
        lax.all_to_all(slot_part, "exp", split_axis=0, concat_axis=1, tiled=True),
        lax.all_to_all(back_part, "exp", split_axis=0, concat_axis=1, tiled=True),
        lax.all_to_all(param_part, "exp", split_axis=0, concat_axis=1, tiled=True),
    )
    totals = lax.psum((partials[0], partials[1], partials[2]), "seq")
    feature_width = slot_param.shape[1]
    offset = lax.axis_index("seq") * feature_width
    shares = tuple((lax.dynamic_slice_in_dim(total, offset, feature_width, 1) for total in totals))
    slot_inputs = shares[0].astype(jnp.bfloat16)
    grad_slot_out = shares[1].astype(jnp.bfloat16)
    grad_param = shares[2].astype(jnp.bfloat16)
    return (slot_inputs, layer_output, grad_tokens, grad_param, grad_slot_out)


def solution(mesh):
    in_specs = (P("seq", "exp"), P("exp", "seq"), P("exp", "seq"), P("seq", "exp"), P("exp", "seq"))
    out_specs = (
        P("exp", "seq"),
        P("seq", "exp"),
        P("seq", "exp"),
        P("exp", "seq"),
        P("exp", "seq"),
    )
    return jax.shard_map(shards, mesh=mesh, in_specs=in_specs, out_specs=out_specs, check_vma=False)
```

profile of v0, /device:TPU:8, one launch (start us, length us, event | category | flops | bytes accessed | tf_op | source)
XLA Modules:
  0.0 1195.2 jit_solution(15656686033707107687)
XLA Ops:
  7.2 106.6 %all-gather = bf16[64,96,32]{1,2,0:T(8,128)(2,1)S(1)} all-gather(bf16[1,96,32]{1,2,0:T(8,128)(2,1)} %bitcast.81), channel_id=1, replica_groups=mesh['seq'=64,'exp'=8] {'seq'}, dimensions={0}, use_global_device_ids=true | all-gather | bytes 399360 | tf_op jit(solution)/shard_map/all_gather | solution.py:21
  115.5 5.0 all-to-all-start
  120.5 98.5 %all-gather.2 = bf16[64,96,32]{1,2,0:T(8,128)(2,1)S(1)} all-gather(bf16[1,96,32]{1,2,0:T(8,128)(2,1)S(1)} %bitcast.82), channel_id=1, replica_groups=mesh['seq'=64,'exp'=8] {'seq'}, dimensions={0}, use_global_device_ids=true | all-gather | bytes 399360 | tf_op jit(solution)/shard_map/all_gather | solution.py:23
  220.7 4.9 all-to-all-start.3
  225.6 97.5 %all-gather.1 = bf16[64,96,32]{1,2,0:T(8,128)(2,1)S(1)} all-gather(bf16[1,96,32]{1,2,0:T(8,128)(2,1)S(1)} %bitcast.83), channel_id=1, replica_groups=mesh['seq'=64,'exp'=8] {'seq'}, dimensions={0}, use_global_device_ids=true | all-gather | bytes 399360 | tf_op jit(solution)/shard_map/all_gather | solution.py:22
  324.9 4.8 all-to-all-start.2
  331.7 5.5 all-to-all-done.2
  338.2 69.4 %all-reduce.5.cloned.1.call-done = (f32[256,256]{1,0:T(8,128)}, f32[256,256]{1,0:T(8,128)}, f32[256,256]{1,0:T(8,128)}) async-done(((f32[256,256]{1,0:T(8,128)}, f32[256,256]{1,0:T(8,128)}, f32[256,256]{1,0:T(8,128)}), (f32[256,256]{1,0:T(8,128)}, f32[256,256]{1,0:T(8,128)}, f32[256,256]{1,0:T(8,128)})) %all-reduce.5.cloned.1.call-update) | async-done | bytes 786448 | tf_op jit(solution)/shard_map/psum | solution.py:30
  408.8 144.1 %pmax.7 = f32[256]{0:T(256)S(1)} all-reduce(f32[256]{0:T(256)S(1)} %get-tuple-element.10), channel_id=1, replica_groups=mesh['seq'=64,'exp'=8] {'seq'}, use_global_device_ids=true, to_apply=%region_2.0 | all-reduce | flops 256 | bytes 2048 | tf_op jit(solution)/shard_map/pmax | solution.py:31
  553.1 138.0 %psum.57 = f32[256]{0:T(256)S(1)} all-reduce(f32[256]{0:T(256)S(1)} %get-tuple-element.8), channel_id=1, replica_groups=mesh['seq'=64,'exp'=8] {'seq'}, use_global_device_ids=true, to_apply=%region_4.0 | all-reduce | flops 256 | bytes 2048 | tf_op jit(solution)/shard_map/psum | solution.py:32
  691.1 1.2 multiply_reduce_fusion.1
  692.3 140.0 %psum.61 = f32[256]{0:T(256)S(1)} all-reduce(f32[256]{0:T(256)S(1)} %get-tuple-element.6), channel_id=1, replica_groups=mesh['seq'=64,'exp'=8] {'seq'}, use_global_device_ids=true, to_apply=%region_12.0 | all-reduce | flops 256 | bytes 2048 | tf_op jit(solution)/shard_map/psum | solution.py:50
  832.5 1.2 fusion.20
  833.7 6.2 all-to-all-start.4
  839.9 1.2 fusion.10
  841.1 10.5 all-to-all-done.4
  851.6 4.9 all-to-all-start.1
  856.5 2.3 fusion.5
  858.8 9.4 all-to-all-done.1
  868.2 5.5 all-to-all-start.5
  876.3 9.3 all-to-all-done.5
  885.6 1.2 copy.36
  886.8 299.5 %all-reduce.6 = (bf16[32,6144]{1,0:T(8,128)(2,1)S(1)}, bf16[32,6144]{1,0:T(8,128)(2,1)S(1)}, bf16[32,6144]{1,0:T(8,128)(2,1)}) all-reduce(f32[32,6144]{1,0:T(8,128)S(1)} %bitcast.72, f32[32,6144]{1,0:T(8,128)S(1)} %bitcast.71, f32[32,6144]{1,0:T(8,128)S(1)} %bitcast.73), channel_id=1, replica_groups=mesh['seq'=64,'exp'=8] {'seq'}, use_global_device_ids=true, to_apply=%region_5.0 | all-reduce | flops 589824 | bytes 3538944 | tf_op jit(solution)/shard_map/psum | solution.py:63
  1186.9 1.4 dynamic-slice_convert_fusion
  (39 shorter events, 12.9 us)
Async XLA Ops:
  7.2 322.5 %copy-start = (bf16[256,768]{1,0:T(8,128)(2,1)S(1)}, bf16[256,768]{1,0:T(8,128)(2,1)}, u32[]{:S(2)}) copy-start(bf16[256,768]{1,0:T(8,128)(2,1)} %param.5) | copy-start | bytes 1179652
  115.5 5.1 copy-start.5
  115.5 105.2 %all-to-all-start = ((bf16[32,8,768]{2,0,1:T(8,128)(2,1)}), bf16[32,8,768]{2,0,1:T(8,128)(2,1)S(1)}, u32[]{:S(2)}, u32[]{:S(2)}) async-start(bf16[32,8,768]{2,0,1:T(8,128)(2,1)} %bitcast.64), calls=%async_computation | async-start | bytes 786432 | tf_op jit(solution)/shard_map/all_to_all | solution.py:26
  220.7 4.9 copy-start.6
  220.7 104.2 %all-to-all-start.3 = ((bf16[32,8,768]{2,0,1:T(8,128)(2,1)}), bf16[32,8,768]{2,0,1:T(8,128)(2,1)S(1)}, u32[]{:S(2)}, u32[]{:S(2)}) async-start(bf16[32,8,768]{2,0,1:T(8,128)(2,1)} %bitcast.62), calls=%async_computation.3 | async-start | bytes 786432 | tf_op jit(solution)/shard_map/all_to_all | solution.py:28
  324.9 12.3 %all-to-all-start.2 = ((bf16[32,8,768]{2,0,1:T(8,128)(2,1)}), bf16[32,8,768]{2,0,1:T(8,128)(2,1)S(1)}, u32[]{:S(2)}, u32[]{:S(2)}) async-start(bf16[32,8,768]{2,0,1:T(8,128)(2,1)} %bitcast.63), calls=%async_computation.2 | async-start | bytes 786432 | tf_op jit(solution)/shard_map/all_to_all | solution.py:27
  329.7 78.0 %all-reduce.5.cloned.1.call-start = ((), (), s32[]{:S(2)}) async-start(), calls=%async_computation.6 | async-start | bytes 1572864 | tf_op jit(solution)/shard_map/psum | solution.py:30
  330.7 6.5 copy-start.4
  407.6 145.3 %copy-start.1 = (f32[256,256]{1,0:T(8,128)S(1)}, f32[256,256]{1,0:T(8,128)}, u32[]{:S(2)}) copy-start(f32[256,256]{1,0:T(8,128)} %get-tuple-element.14) | copy-start | bytes 786436
  407.6 283.4 %copy-start.2 = (f32[256,256]{1,0:T(8,128)S(1)}, f32[256,256]{1,0:T(8,128)}, u32[]{:S(2)}) copy-start(f32[256,256]{1,0:T(8,128)} %get-tuple-element.15) | copy-start | bytes 786436
  691.1 141.2 %copy-start.3 = (f32[256,256]{1,0:T(8,128)S(1)}, f32[256,256]{1,0:T(8,128)}, u32[]{:S(2)}) copy-start(f32[256,256]{1,0:T(8,128)} %get-tuple-element.16) | copy-start | bytes 786436
  833.7 17.9 %all-to-all-start.4 = ((f32[8,32,768]{2,1,0:T(8,128)}), f32[8,32,768]{2,1,0:T(8,128)S(1)}, u32[]{:S(2)}, u32[]{:S(2)}) async-start(f32[8,32,768]{2,1,0:T(8,128)} %bitcast.20), calls=%async_computation.4 | async-start | bytes 1572864 | tf_op jit(solution)/shard_map/all_to_all | solution.py:61
  851.6 16.6 %all-to-all-start.1 = ((f32[8,32,768]{2,1,0:T(8,128)}), f32[8,32,768]{2,1,0:T(8,128)S(1)}, u32[]{:S(2)}, u32[]{:S(2)}) async-start(f32[8,32,768]{2,1,0:T(8,128)} %bitcast.79), calls=%async_computation.1 | async-start | bytes 1572864 | tf_op jit(solution)/shard_map/all_to_all | solution.py:59
  868.2 17.4 %all-to-all-start.5 = ((f32[8,32,768]{2,1,0:T(8,128)}), f32[8,32,768]{2,1,0:T(8,128)}, u32[]{:S(2)}, u32[]{:S(2)}) async-start(f32[8,32,768]{2,1,0:T(8,128)} %bitcast.80), calls=%async_computation.5 | async-start | bytes 1572864 | tf_op jit(solution)/shard_map/all_to_all | solution.py:60
Sparse Core Ops, SparseCore 0:
  338.3 69.2 all-reduce.4
where the time goes:
time: 1200 us
  blocking collectives  1020 us (85%)
  waiting for transfers between devices  104 us (9%)
  starting transfers between devices  31.4 us (3%)
  between operations  14.1 us (1%)
    psum x1, blocking collectives, shards(): totals = lax.psum((partials[0], partials[1], partials[2]), 'seq')  299 us
    pmax x1, blocking collectives, shards(): col_max = lax.pmax(jnp.max(logits, axis=0), 'seq')  144 us
    psum x1, blocking collectives, shards(): column_sum = lax.psum(jnp.sum(dispatch_full * grad_dispatch, axis=0), 'seq')  140 us
    psum x1, blocking collectives, shards(): col_total = lax.psum(jnp.sum(jnp.exp(logits - col_max), axis=0), 'seq')  138 us
    all_gather x1, blocking collectives, shards(): lax.all_gather(slot_param, 'seq', axis=1, tiled=True)  107 us
    all_gather x1, blocking collectives, shards(): lax.all_gather(grad_slot_in, 'seq', axis=1, tiled=True)  98.5 us
    all_gather x1, blocking collectives, shards(): lax.all_gather(slot_outputs, 'seq', axis=1, tiled=True)  97.5 us
    psum x1, waiting for transfers between devices, shards(): logits = lax.psum(contract_last(tokens, param_cols), 'exp')  69.4 us
  transfers between devices with their start and end apart: 7, of which 5 were waited for; matrix products, arithmetic and copies ran while one was open for 1% of the time, Pallas kernels for 0%

commit v1 on v0

v1 whole, which is shorter than its diff:
```python
import functools

import jax
import jax.numpy as jnp
from jax import lax
from jax.experimental import pallas as pl
from jax.experimental.pallas import tpu as pltpu
from jax.sharding import PartitionSpec as P

MESH = pl.DeviceIdType.MESH
F32 = jnp.float32
BF16 = jnp.bfloat16

NEAR = [(dx, dz) for dz in (2, 1, -1, 0) for dx in (2, 1, 3, 0) if (dx, dz) != (0, 0)]
FAR = [8, 4, -4]
GROUP = [(dy, dc) for dy in (2, 1, 3, 0) for dc in (1, 0) if (dy, dc) != (0, 0)]
PARAM, COTAN, OUTPUT = 0, 1, 2
BACK, SLOT, GPARAM = 0, 1, 2


def rows_by_rows(left, right):
    return lax.dot_general(left, right, (((1,), (1,)), ((), ())), preferred_element_type=F32)


def columns_by_columns(left, right):
    return lax.dot_general(left, right, (((0,), (0,)), ((), ())), preferred_element_type=F32)


def dot(left, right):
    return jnp.dot(left, right, preferred_element_type=F32)


def kernel(
    tok_ref, par_ref, out_ref, go_ref, gsi_ref,
    slot_in_ref, layer_ref, gtok_ref, gpar_ref, gso_ref,
    blk, w, tp, gp, part, red, mine, full, st_m, st_u, far_m, far_u, comb, q, r1, hold, coll,
    sp_s, sp_r, ag_s, ag_r, rs_s, rs_r, eg_s, eg_r, nm_s, nm_r, fm_s, fm_r, p1_s, p1_r, p2_s, p2_r,
):
    s, e = lax.axis_index("seq"), lax.axis_index("exp")
    x, z = s // 16, s % 16
    y, c = e // 2, e % 2
    k = z % 4
    two = 2 - 4 * c

    def near_of(dx, dz):
        dz = two if dz == 2 else dz
        return (x + dx) % 4, (z + dz + 16) % 16

    def near_id(dx, dz):
        nx, nz = near_of(dx, dz)
        return (nx * 16 + nz, e)

    def near_source(dx, dz):
        dz = two if dz == 2 else dz
        return (x - dx + 4) % 4, (z - dz + 16) % 16

    def far_id(dz):
        return (x * 16 + (z + dz + 16) % 16, e)

    def group_id(dy, dc):
        return (s, ((y + dy) % 4) * 2 + (c + dc) % 2)

    h_me = (z % 8) // 4

    def holder_id(g):
        return (y * 16 + (z + 4 * g) % 16, x * 2 + z // 8)

    own_self = (y == x) & (c == z // 8)

    def owner_id(h, cc):
        return (y * 16 + 8 * c + 4 * h + k, x * 2 + cc)

    def holder_g(h):
        return (z // 4 - 2 * c - h + 8) % 4

    def owner_is_self(h, cc):
        return (x == y) & (z == 8 * c + 4 * h + k) & (c == cc)

    barrier = pltpu.get_barrier_semaphore()

    def greet(device):
        pl.semaphore_signal(barrier, inc=1, device_id=device, device_id_type=MESH)

    for g in (2, 1, 3):
        greet(holder_id(g))

    @pl.when(jnp.logical_not(own_self))
    def _():
        greet(holder_id(0))

    for h in (0, 1):
        for cc in (0, 1):
            @pl.when(jnp.logical_not(owner_is_self(h, cc)))
            def _():
                greet(owner_id(h, cc))

    for dz in FAR:
        greet(far_id(dz))
    for o in NEAR:
        nx, nz = near_source(*o)
        greet((nx * 16 + nz, e))
    for o in GROUP:
        greet(group_id(*o))

    blk[...] = jnp.zeros_like(blk)
    blk[PARAM, :, 0:96] = par_ref[...]
    blk[COTAN, :, 0:96] = gsi_ref[...]
    blk[OUTPUT, :, 0:96] = out_ref[...]
    for src, dst in ((tok_ref, tp), (go_ref, gp)):
        dst[...] = jnp.zeros_like(dst)
        for j in range(8):
            j2 = 2 * (j % 4) + j // 4
            dst[:, 128 * j2:128 * j2 + 96] = src[:, 96 * j:96 * j + 96]

    pl.semaphore_wait(barrier, len(FAR) + len(NEAR) + len(GROUP) + 8 - 2 * own_self.astype(jnp.int32))

    sent = []

    def send(src, dst, ss, rs, device, unless=None):
        cp = pltpu.make_async_remote_copy(
            src_ref=src, dst_ref=dst, send_sem=ss, recv_sem=rs, device_id=device, device_id_type=MESH
        )
        if unless is None:
            cp.start()
        else:
            pl.when(jnp.logical_not(unless))(cp.start)
        sent.append((unless, cp))

    def receive(ref, ss, rs, unless=None):
        cp = pltpu.make_async_remote_copy(
            src_ref=ref, dst_ref=ref, send_sem=ss, recv_sem=rs, device_id=near_id(1, 0), device_id_type=MESH
        )
        if unless is None:
            cp.wait_recv()
        else:
            pl.when(jnp.logical_not(unless))(cp.wait_recv)

    own_row = pl.multiple_of(64 * y + 32 * c, 32)
    own_col = pl.multiple_of(128 * (2 * k + h_me), 128)
    for a in (PARAM, COTAN, OUTPUT):
        spot = w.at[a, pl.ds(own_row, 32), pl.ds(own_col, 128)]
        for g in (2, 1, 3):
            send(blk.at[a], spot, sp_s.at[a, g], sp_r.at[a, 2 * h_me + c], holder_id(g))
        send(blk.at[a], spot, sp_s.at[a, 0], sp_r.at[a, 2 * h_me + c], holder_id(0), own_self)

        @pl.when(own_self)
        def _():
            w[a, pl.ds(own_row, 32), pl.ds(own_col, 128)] = blk[a]

    held_row = pl.multiple_of(64 * x, 64)
    held_col = pl.multiple_of(256 * k, 256)
    for a in (PARAM, COTAN, OUTPUT):
        for h in (0, 1):
            for cc in (0, 1):
                spot = w.at[a, pl.ds(held_row + 32 * cc, 32), pl.ds(held_col + 128 * h, 128)]
                receive(spot, sp_s.at[a, 0], sp_r.at[a, 2 * h + cc], owner_is_self(h, cc))
        spot = w.at[a, pl.ds(held_row, 64), pl.ds(held_col, 256)]
        for i, o in enumerate(NEAR):
            send(spot, spot, ag_s.at[a, i], ag_r.at[a, i], near_id(*o))

    def gathered(a):
        for i, (dx, dz) in enumerate(NEAR):
            nx, nz = near_source(dx, dz)
            spot = w.at[
                a,
                pl.ds(pl.multiple_of(64 * nx, 64), 64),
                pl.ds(pl.multiple_of(256 * (nz % 4), 256), 256),
            ]
            receive(spot, ag_s.at[a, i], ag_r.at[a, i])

    def scatter(a):
        for i, o in enumerate(GROUP):
            device = group_id(*o)
            spot = part.at[a, pl.ds(pl.multiple_of(32 * device[1], 32), 32)]
            send(spot, red.at[a, i], rs_s.at[a, i], rs_r.at[a, i], device)

    my_tok = pl.multiple_of(32 * e, 32)

    def gather(a):
        total = part[a, pl.ds(my_tok, 32), :]
        for i in range(len(GROUP)):
            receive(red.at[a, i], rs_s.at[a, i], rs_r.at[a, i])
            total = total + red[a, i]
        mine[a] = total
        full[a, pl.ds(my_tok, 32), :] = total
        for i, o in enumerate(GROUP):
            send(mine.at[a], full.at[a, pl.ds(my_tok, 32)], eg_s.at[a, i], eg_r.at[a, i], group_id(*o))

    def complete(a):
        for i, (dy, dc) in enumerate(GROUP):
            ee = ((y - dy + 4) % 4) * 2 + (c + dc) % 2
            spot = full.at[a, pl.ds(pl.multiple_of(32 * ee, 32), 32)]
            receive(spot, eg_s.at[a, i], eg_r.at[a, i])

    gathered(PARAM)
    part[PARAM] = rows_by_rows(tp[...], w[PARAM])
    scatter(PARAM)
    gathered(COTAN)
    part[COTAN] = rows_by_rows(tp[...], w[COTAN])
    scatter(COTAN)
    gather(PARAM)
    gathered(OUTPUT)
    part[OUTPUT] = rows_by_rows(gp[...], w[OUTPUT])
    scatter(OUTPUT)
    gather(COTAN)
    complete(PARAM)

    logits = full[0]
    col_max = jnp.max(logits, axis=0, keepdims=True)
    expo = jnp.exp(logits - col_max)
    col_total = jnp.sum(expo, axis=0, keepdims=True)
    n = len(NEAR)
    st_m[n, 0:1] = col_max
    st_m[n, 1:2] = col_total
    for i, o in enumerate(NEAR):
        send(st_m.at[n], st_m.at[i], nm_s.at[0, i], nm_r.at[0, i], near_id(*o))

    row_max = jnp.max(logits, axis=1, keepdims=True)
    weights = jnp.exp(logits - row_max)
    combine_full = weights / jnp.sum(weights, axis=1, keepdims=True)
    comb[...] = combine_full
    combine = combine_full.astype(BF16)

    def partial(a, left, right_ref):
        left_t = left.T
        for kk in range(4):
            q[a, :, 256 * kk:256 * kk + 256] = dot(left_t, right_ref[:, 256 * kk:256 * kk + 256]).astype(BF16)
        for i, (dx, dz) in enumerate(NEAR):
            nx, nz = near_of(dx, dz)
            spot = q.at[
                a,
                pl.ds(pl.multiple_of(64 * nx, 64), 64),
                pl.ds(pl.multiple_of(256 * (nz % 4), 256), 256),
            ]
            send(spot, r1.at[a, i], p1_s.at[a, i], p1_r.at[a, i], near_id(dx, dz))

    def unpad(dst, j_value):
        for kk in range(4):
            value = j_value(kk).astype(BF16)
            for h in (0, 1):
                j = 4 * h + kk
                dst[:, 96 * j:96 * j + 96] = value[:, 128 * h:128 * h + 96]

    gather(OUTPUT)
    partial(BACK, combine, gp)

    complete(COTAN)
    expo = jnp.exp(full[0] - st_m[n, 0:1])
    st_u[n, 0:1] = jnp.sum(expo * full[COTAN], axis=0, keepdims=True)
    st_u[n, 1:2] = jnp.zeros((1, 256), F32)
    for i, o in enumerate(NEAR):
        send(st_u.at[n], st_u.at[i], nm_s.at[1, i], nm_r.at[1, i], near_id(*o))

    for i in range(n):
        receive(st_m.at[i], nm_s.at[0, i], nm_r.at[0, i])
    near_max = st_m[n, 0:1]
    for i in range(n):
        near_max = jnp.maximum(near_max, st_m[i, 0:1])
    near_total = jnp.zeros((1, 256), F32)
    factors = []
    for i in range(n + 1):
        factor = jnp.exp(st_m[i, 0:1] - near_max)
        factors.append(factor)
        near_total = near_total + factor * st_m[i, 1:2]
    far_m[3, 0:1] = near_max
    far_m[3, 1:2] = near_total
    for i, dz in enumerate(FAR):
        send(far_m.at[3], far_m.at[i], fm_s.at[0, i], fm_r.at[0, i], far_id(dz))

    for i in range(n):
        receive(st_u.at[i], nm_s.at[1, i], nm_r.at[1, i])
    near_inner = jnp.zeros((1, 256), F32)
    for i in range(n + 1):
        near_inner = near_inner + factors[i] * st_u[i, 0:1]
    far_u[3, 0:1] = near_inner
    far_u[3, 1:2] = jnp.zeros((1, 256), F32)
    for i, dz in enumerate(FAR):
        send(far_u.at[3], far_u.at[i], fm_s.at[1, i], fm_r.at[1, i], far_id(dz))

    complete(OUTPUT)
    unpad(layer_ref, lambda kk: dot(comb[...].astype(BF16), w[OUTPUT, :, 256 * kk:256 * kk + 256]))

    for i in range(3):
        receive(far_m.at[i], fm_s.at[0, i], fm_r.at[0, i])
    col_max = jnp.maximum(
        jnp.maximum(far_m[0, 0:1], far_m[1, 0:1]), jnp.maximum(far_m[2, 0:1], far_m[3, 0:1])
    )
    col_total = jnp.zeros((1, 256), F32)
    factors = []
    for i in range(4):
        factor = jnp.exp(far_m[i, 0:1] - col_max)
        factors.append(factor)
        col_total = col_total + factor * far_m[i, 1:2]
    dispatch_full = jnp.exp(full[0] - col_max) / col_total
    dispatch = dispatch_full.astype(BF16)
    partial(SLOT, dispatch, tp)

    for i in range(3):
        receive(far_u.at[i], fm_s.at[1, i], fm_r.at[1, i])
    inner = jnp.zeros((1, 256), F32)
    for i in range(4):
        inner = inner + factors[i] * far_u[i, 0:1]
    inner = inner / col_total
    combine_full = comb[...]
    grad_combine = full[OUTPUT]
    from_combine = combine_full * (
        grad_combine - jnp.sum(combine_full * grad_combine, axis=1, keepdims=True)
    )
    from_dispatch = dispatch_full * (full[COTAN] - inner)
    grad_logits = (from_combine + from_dispatch).astype(BF16)
    partial(GPARAM, grad_logits, tp)

    def to_owners(a):
        mx = pl.multiple_of(64 * x, 64)
        mk = pl.multiple_of(256 * k, 256)
        total = q[a, pl.ds(mx, 64), pl.ds(mk, 256)].astype(F32)
        for i in range(n):
            receive(r1.at[a, i], p1_s.at[a, i], p1_r.at[a, i])
            total = total + r1[a, i].astype(F32)
        total = total.astype(BF16)
        for h in (0, 1):
            for cc in (0, 1):
                hold[a, 2 * h + cc] = total[32 * cc:32 * cc + 32, 128 * h:128 * h + 128]
        for h in (0, 1):
            for cc in (0, 1):
                i = 2 * h + cc
                here = owner_is_self(h, cc)
                g = holder_g(h)
                send(hold.at[a, i], coll.at[a, g], p2_s.at[a, i], p2_r.at[a, g], owner_id(h, cc), here)

                @pl.when(here)
                def _():
                    coll[a, g] = hold[a, i]

    to_owners(BACK)
    to_owners(SLOT)
    unpad(
        gtok_ref,
        lambda kk: dot(dispatch, w[COTAN, :, 256 * kk:256 * kk + 256])
        + dot(grad_logits, w[PARAM, :, 256 * kk:256 * kk + 256]),
    )
    to_owners(GPARAM)

    for a, ref in ((BACK, gso_ref), (SLOT, slot_in_ref), (GPARAM, gpar_ref)):
        for g in range(4):
            receive(coll.at[a, g], p2_s.at[a, 0], p2_r.at[a, g], own_self if g == 0 else None)
        total = coll[a, 0].astype(F32)
        for g in range(1, 4):
            total = total + coll[a, g].astype(F32)
        ref[...] = total.astype(BF16)[:, 0:96]

    for unless, cp in sent:
        if unless is None:
            cp.wait_send()
        else:
            pl.when(jnp.logical_not(unless))(cp.wait_send)


def shards(tokens, slot_param, slot_outputs, grad_output, grad_slot_in):
    n, f, m = len(NEAR), len(FAR), len(GROUP)
    dma = pltpu.SemaphoreType.DMA
    vmem = pl.BlockSpec(memory_space=pltpu.VMEM)
    slot_in, layer, gtok, gpar, gso = pl.pallas_call(
        kernel,
        out_shape=[
            jax.ShapeDtypeStruct((32, 96), BF16),
            jax.ShapeDtypeStruct((256, 768), BF16),
            jax.ShapeDtypeStruct((256, 768), BF16),
            jax.ShapeDtypeStruct((32, 96), BF16),
            jax.ShapeDtypeStruct((32, 96), BF16),
        ],
        in_specs=[vmem] * 5,
        out_specs=[vmem] * 5,
        scratch_shapes=[
            pltpu.VMEM((3, 32, 128), BF16),
            pltpu.VMEM((3, 256, 1024), BF16),
            pltpu.VMEM((256, 1024), BF16),
            pltpu.VMEM((256, 1024), BF16),
            pltpu.VMEM((3, 256, 256), F32),
            pltpu.VMEM((3, m, 32, 256), F32),
            pltpu.VMEM((3, 32, 256), F32),
            pltpu.VMEM((3, 256, 256), F32),
            pltpu.VMEM((n + 1, 2, 256), F32),
            pltpu.VMEM((n + 1, 2, 256), F32),
            pltpu.VMEM((f + 1, 2, 256), F32),
            pltpu.VMEM((f + 1, 2, 256), F32),
            pltpu.VMEM((256, 256), F32),
            pltpu.VMEM((3, 256, 1024), BF16),
            pltpu.VMEM((3, n, 64, 256), BF16),
            pltpu.VMEM((3, 4, 32, 128), BF16),
            pltpu.VMEM((3, 4, 32, 128), BF16),
            dma((3, 4)), dma((3, 4)),
            dma((3, n)), dma((3, n)),
            dma((3, m)), dma((3, m)),
            dma((3, m)), dma((3, m)),
            dma((2, n)), dma((2, n)),
            dma((2, f)), dma((2, f)),
            dma((3, n)), dma((3, n)),
            dma((3, 4)), dma((3, 4)),
        ],
        compiler_params=pltpu.CompilerParams(
            collective_id=0, has_side_effects=True, vmem_limit_bytes=40 * 1024 * 1024
        ),
        cost_estimate=pl.CostEstimate(flops=10**9, bytes_accessed=2 * 10**6, transcendentals=10**5),
        name="soft_moe",
    )(tokens, slot_param, slot_outputs, grad_output, grad_slot_in)
    return slot_in, layer, gtok, gpar, gso


def solution(mesh):
    by_seq, by_exp = P("seq", "exp"), P("exp", "seq")
    return jax.shard_map(
        shards,
        mesh=mesh,
        in_specs=(by_seq, by_exp, by_exp, by_seq, by_exp),
        out_specs=(by_exp, by_seq, by_seq, by_exp, by_exp),
        check_vma=False,
    )
```

time: 1200 us -> 103 us (0.09)
  the two profiles are of different devices: /device:TPU:8 before, /device:TPU:1 now
where the time goes in v1:
time: 103 us; the launch traced here: 102 us
  Pallas kernels  94.1 us (91%)
  local copies, waits for them, and re-layouts  7.36 us (7%)
    pallas_call x1, Pallas kernels, shards(): pl.pallas_call(kernel, out_shape=[jax.ShapeDtypeStruct((32, 96), BF16), j...  94.1 us
    unnamed x15, local copies, waits for them, and re-layouts  7.36 us

profile of v1, /device:TPU:1, one launch (start us, length us, event | category | flops | bytes accessed | tf_op | source)
XLA Modules:
  0.0 102.1 jit_solution(13279316344642779917)
XLA Ops:
  0.6 0.0 copy-start
  0.6 1.0 copy-done
  1.6 0.0 copy-start.1
  1.6 1.0 copy-done.1
  2.6 0.0 copy-start.2
  2.6 0.7 copy-done.2
  3.3 0.0 copy-start.3
  3.3 0.7 copy-done.3
  4.0 0.0 copy-start.4
  4.0 0.7 copy-done.4
  4.7 94.1 %soft_moe.1 = (bf16[32,96]{1,0:T(8,128)(2,1)S(1)}, bf16[256,768]{1,0:T(8,128)(2,1)S(1)}, bf16[256,768]{1,0:T(8,128)(2,1)S(1)}, bf16[32,96]{1,0:T(8,128)(2,1)S(1)}, bf16[32,96]{1,0:T(8,128)(2,1)S(1)}) custom-call(bf16[256,768]{1,0:T(8,128)(2,1)S(1)} %copy-done, bf16[32,96]{1,0:T(8,128)(2,1)S(1)} %copy-done.2, bf16[32,96]{1,0:T(8,128)(2,1)S(1)} %copy-done.3, ...), custom_call_target="tpu_custom_call" | custom-call | flops 1000000000 | bytes 2000000 | tf_op jit(solution)/shard_map/soft_moe/pallas_call | solution.py:363
  98.8 0.6 copy.15
  99.4 0.7 copy.16
  100.1 0.7 copy.17
  100.9 0.6 copy.18
  101.5 0.6 copy.19
Async XLA Ops:
  0.6 1.0 copy-start
  1.6 1.0 copy-start.1
  2.6 0.7 copy-start.2
  3.3 0.7 copy-start.3
  4.0 0.7 copy-start.4

commit v2 on v0

v2 whole, which is shorter than its diff:
```python
import jax
import jax.numpy as jnp
from jax import lax
from jax.experimental import pallas as pl
from jax.experimental.pallas import tpu as pltpu
from jax.sharding import PartitionSpec as P

MESH = pl.DeviceIdType.MESH
F32 = jnp.float32
BF16 = jnp.bfloat16

NEAR = [(dx, dz) for dz in (2, 1, -1, 0) for dx in (2, 1, 3, 0) if (dx, dz) != (0, 0)]
FAR = [8, 4, -4]
GROUP = [(dy, dc) for dy in (2, 1, 3, 0) for dc in (1, 0) if (dy, dc) != (0, 0)]
N, M, L = len(NEAR), len(GROUP), len(FAR)
PARAM, COTAN, OUTPUT = 0, 1, 2
BACK, SLOT, GPARAM = 0, 1, 2


def rows_by_rows(left, right):
    return lax.dot_general(left, right, (((1,), (1,)), ((), ())), preferred_element_type=F32)


def dot(left, right):
    return jnp.dot(left, right, preferred_element_type=F32)


def kernel(
    tok_hbm, par_hbm, out_hbm, go_hbm, gsi_hbm,
    slot_in_hbm, layer_hbm, gtok_hbm, gpar_hbm, gso_hbm,
    layer_ref, gtok_ref, owned, tok, go, small, blk, inbox, w, tok_t, go_t, part, red, full,
    grp_m, grp_u, st_m, st_u, far_m, far_u, col_stats, comb, from_combine, disp, q, r1, hold, coll,
    in_sem, out_sem, sp_s, sp_r, wf_s, wf_r, ag_s, ag_r, rs_s, rs_r, eg_s, eg_r,
    gm_s, gm_r, nm_s, nm_r, fm_s, fm_r, p1_s, p1_r, p2_s, p2_r,
):
    s, e = lax.axis_index("seq"), lax.axis_index("exp")
    x, z = s // 16, s % 16
    y, c = e // 2, e % 2
    two = 2 - 4 * c

    loads = [
        pltpu.make_async_copy(src, dst, in_sem.at[i])
        for i, (src, dst) in enumerate((
            (par_hbm, small.at[PARAM]), (gsi_hbm, small.at[COTAN]), (out_hbm, small.at[OUTPUT]),
            (tok_hbm, tok), (go_hbm, go),
        ))
    ]
    for load in loads:
        load.start()

    def near_of(dx, dz):
        dz = two if dz == 2 else dz
        return (x + dx) % 4, (z + dz + 16) % 16

    def near_id(dx, dz):
        nx, nz = near_of(dx, dz)
        return (nx * 16 + nz, e)

    def near_source(dx, dz):
        dz = two if dz == 2 else dz
        return (x - dx + 4) % 4, (z - dz + 16) % 16

    def far_id(dz):
        return (x * 16 + (z + dz + 16) % 16, e)

    def group_id(dy, dc):
        return (s, ((y + dy) % 4) * 2 + (c + dc) % 2)

    def block_of(bx, bz):
        row = pl.multiple_of(96 * (4 * (bx % 2) + bz % 4), 32)
        col = pl.multiple_of(128 * (bx // 2), 128)
        return pl.ds(row, 96), pl.ds(col, 128)

    own_block = block_of(x, z)
    is_primary = z // 4 == 2 * c + x % 2
    not_primary = jnp.logical_not(is_primary)
    primary_id = (x * 16 + 8 * c + 4 * (x % 2) + z % 4, e)
    home_id = ((2 * (y // 2) + (z % 8) // 4) * 16 + z, 2 * x + z // 8)
    home_self = (x == y) & is_primary
    place = 2 * (y % 2) + c

    def owner_id(i):
        return (y * 16 + z, 2 * (2 * (x // 2) + i // 2) + i % 2)

    def owner_self(i):
        return (x == y) & (y == 2 * (x // 2) + i // 2) & (c == i % 2)

    barrier = pltpu.get_barrier_semaphore()

    def greet(device):
        pl.semaphore_signal(barrier, inc=1, device_id=device, device_id_type=MESH)

    for dz in FAR:
        greet(far_id(dz))
    pl.when(jnp.logical_not(home_self))(lambda: greet(home_id))
    for i in range(4):
        pl.when(is_primary & jnp.logical_not(owner_self(i)))(lambda i=i: greet(owner_id(i)))
    for o in NEAR:
        nx, nz = near_source(*o)
        greet((nx * 16 + nz, e))
    for o in GROUP:
        greet(group_id(*o))

    for i in range(3):
        loads[i].wait()
    blk[...] = jnp.zeros_like(blk)
    for a in range(3):
        blk[32 * a:32 * a + 32, 0:96] = small[a]
    loads[3].wait()
    tok_t[...] = tok[...].T
    loads[4].wait()
    go_t[...] = go[...].T

    pl.semaphore_wait(
        barrier,
        N + M + L + 1 + 4 * is_primary.astype(jnp.int32) - 2 * home_self.astype(jnp.int32),
    )

    sent = []

    def drain(keep=0):
        while len(sent) > keep:
            wait, when = sent.pop(0)
            if when is None:
                wait()
            else:
                pl.when(when)(wait)

    def copy(src, dst, ss, rs, device=None):
        return pltpu.make_async_remote_copy(
            src_ref=src, dst_ref=dst, send_sem=ss, recv_sem=rs,
            device_id=near_id(1, 0) if device is None else device, device_id_type=MESH,
        )

    def send(copies, whole, ss, rs, when=None):
        def start():
            for src, dst, device in copies:
                copy(src, dst, ss, rs, device).start()

        if when is None:
            start()
        else:
            pl.when(when)(start)
        sent.append((copy(whole, whole, ss, rs).wait_send, when))

    def receive(whole, ss, rs, when=None):
        wait = copy(whole, whole, ss, rs).wait_recv
        if when is None:
            wait()
        else:
            pl.when(when)(wait)

    send([(blk, inbox.at[place], home_id)], blk, sp_s, sp_r.at[place], jnp.logical_not(home_self))

    @pl.when(home_self)
    def _():
        inbox[place] = blk[...]

    @pl.when(is_primary)
    def _():
        for i in range(4):
            receive(inbox.at[i], sp_s, sp_r.at[i], jnp.logical_not(owner_self(i)))

    def pass_on(a):
        spot = w.at[a, *own_block]
        receive(spot, wf_s.at[a], wf_r.at[a], not_primary)
        send([(spot, spot, near_id(*o)) for o in NEAR], r1.at[a], ag_s.at[a], ag_r.at[a])

    for a in (PARAM, COTAN, OUTPUT):
        spot = w.at[a, *own_block]

        @pl.when(is_primary)
        def _():
            rows = jnp.concatenate([inbox[i, 32 * a:32 * a + 32] for i in range(4)], axis=0)
            w[a, *own_block] = rows.astype(F32).T[0:96].astype(BF16)

        send(
            [(spot, spot, far_id(dz)) for dz in FAR], r1.at[a, pl.ds(0, L)], wf_s.at[a], wf_r.at[a], is_primary
        )
        if a != OUTPUT:
            pass_on(a)

    def gathered(a):
        receive(r1.at[a], ag_s.at[a], ag_r.at[a])

    my_tok = pl.multiple_of(32 * e, 32)

    def scatter(a):
        copies = []
        for i, o in enumerate(GROUP):
            device = group_id(*o)
            spot = part.at[a, pl.ds(pl.multiple_of(32 * device[1], 32), 32)]
            copies.append((spot, red.at[a, i], device))
        send(copies, red.at[a], rs_s.at[a], rs_r.at[a])

    def reduced(a):
        total = part[a, pl.ds(my_tok, 32), :]
        receive(red.at[a], rs_s.at[a], rs_r.at[a])
        for i in range(M):
            total = total + red[a, i]
        full[a, pl.ds(my_tok, 32), :] = total
        return total

    def gather(a):
        spot = full.at[a, pl.ds(my_tok, 32)]
        send([(spot, spot, group_id(*o)) for o in GROUP], red.at[a], eg_s.at[a], eg_r.at[a])

    def complete(a):
        receive(red.at[a], eg_s.at[a], eg_r.at[a])

    def spread(buf, ss, rs, ids, t):
        last = buf.shape[0] - 1
        copies = [(buf.at[last], buf.at[i], device) for i, device in enumerate(ids)]
        send(copies, buf.at[pl.ds(0, last)], ss.at[t], rs.at[t])

    def arrived(buf, ss, rs, t):
        receive(buf.at[pl.ds(0, buf.shape[0] - 1)], ss.at[t], rs.at[t])

    def merge(buf):
        count = buf.shape[0]
        top = buf[0, 0:1]
        for i in range(1, count):
            top = jnp.maximum(top, buf[i, 0:1])
        factors = [jnp.exp(buf[i, 0:1] - top) for i in range(count)]
        total = factors[0] * buf[0, 1:2]
        for i in range(1, count):
            total = total + factors[i] * buf[i, 1:2]
        return top, total, factors

    def merge_inner(buf, factors):
        total = factors[0] * buf[0]
        for i in range(1, buf.shape[0]):
            total = total + factors[i] * buf[i]
        return total

    group_ids = [group_id(*o) for o in GROUP]
    near_ids = [near_id(*o) for o in NEAR]
    far_ids = [far_id(dz) for dz in FAR]

    def partial(a, left_t, right):
        for r in range(3):
            q[a, 256 * r:256 * r + 256, :] = dot(left_t[256 * r:256 * r + 256, :], right).astype(BF16)

    def partial_out(a):
        copies = [(q.at[a, *block_of(*near_of(*o))], r1.at[a, i], near_id(*o)) for i, o in enumerate(NEAR)]
        send(copies, r1.at[a], p1_s.at[a], p1_r.at[a])

    gathered(PARAM)
    part[PARAM] = dot(tok[...], w[PARAM])
    scatter(PARAM)
    pass_on(OUTPUT)
    gathered(COTAN)
    part[COTAN] = dot(tok[...], w[COTAN])
    scatter(COTAN)

    own_logits = reduced(PARAM)
    own_max = jnp.max(own_logits, axis=0, keepdims=True)
    own_exp = jnp.exp(own_logits - own_max)
    grp_m[M, 0:1] = own_max
    grp_m[M, 1:2] = jnp.sum(own_exp, axis=0, keepdims=True)
    spread(grp_m, gm_s, gm_r, group_ids, 0)
    gather(PARAM)
    drain(5)

    arrived(grp_m, gm_s, gm_r, 0)
    group_max, group_total, group_factors = merge(grp_m)
    st_m[N, 0:1] = group_max
    st_m[N, 1:2] = group_total
    spread(st_m, nm_s, nm_r, near_ids, 0)

    own_grad = reduced(COTAN)
    grp_u[M] = jnp.sum(own_exp * own_grad, axis=0, keepdims=True)
    spread(grp_u, gm_s, gm_r, group_ids, 1)

    gathered(OUTPUT)
    part[OUTPUT] = dot(go[...], w[OUTPUT])
    scatter(OUTPUT)
    gather(COTAN)

    complete(PARAM)
    logits = full[PARAM]
    weights = jnp.exp(logits - jnp.max(logits, axis=1, keepdims=True))
    comb[...] = weights / jnp.sum(weights, axis=1, keepdims=True)
    partial(BACK, go_t, comb[...].astype(BF16))

    arrived(grp_u, gm_s, gm_r, 1)
    st_u[N] = merge_inner(grp_u, group_factors)
    spread(st_u, nm_s, nm_r, near_ids, 1)

    arrived(st_m, nm_s, nm_r, 0)
    near_max, near_total, near_factors = merge(st_m)
    far_m[L, 0:1] = near_max
    far_m[L, 1:2] = near_total
    spread(far_m, fm_s, fm_r, far_ids, 0)
    partial_out(BACK)

    partial(SLOT, tok_t, jnp.exp(full[PARAM] - group_max).astype(BF16))
    drain(4)

    reduced(OUTPUT)
    gather(OUTPUT)

    arrived(st_u, nm_s, nm_r, 1)
    far_u[L] = merge_inner(st_u, near_factors)
    spread(far_u, fm_s, fm_r, far_ids, 1)
    partial_out(SLOT)

    complete(COTAN)
    complete(OUTPUT)
    combine_full = comb[...]
    grad_combine = full[OUTPUT]
    from_combine[...] = combine_full * (
        grad_combine - jnp.sum(combine_full * grad_combine, axis=1, keepdims=True)
    )

    arrived(far_m, fm_s, fm_r, 0)
    col_max, col_total, far_factors = merge(far_m)
    col_stats[0:1] = col_max
    col_stats[1:2] = col_total
    disp[...] = jnp.exp(full[PARAM] - col_max) / col_total
    drain(2)

    arrived(far_u, fm_s, fm_r, 1)
    inner = merge_inner(far_u, far_factors) / col_total
    grad_logits = (from_combine[...] + disp[...] * (full[COTAN] - inner)).astype(BF16)
    partial(GPARAM, tok_t, grad_logits)
    partial_out(GPARAM)

    stores = [
        pltpu.make_async_copy(src, dst, out_sem.at[i])
        for i, (src, dst) in enumerate((
            (owned.at[BACK], gso_hbm), (owned.at[SLOT], slot_in_hbm), (owned.at[GPARAM], gpar_hbm),
            (layer_ref, layer_hbm), (gtok_ref, gtok_hbm),
        ))
    ]
    layer_ref[...] = rows_by_rows(comb[...].astype(BF16), w[OUTPUT]).astype(BF16)
    stores[3].start()
    gtok_ref[...] = (
        rows_by_rows(disp[...].astype(BF16), w[COTAN]) + rows_by_rows(grad_logits, w[PARAM])
    ).astype(BF16)
    stores[4].start()

    distance = (z // 4 - 2 * c - x % 2 + 4) % 4
    home_z = 8 * c + 4 * (x % 2) + z % 4
    hold[...] = jnp.zeros_like(hold)
    for a in (BACK, SLOT, GPARAM):
        if a == SLOT:
            half = own_block[1]
            scale = [
                jnp.exp(st_m[i, 0:1, half] - col_stats[0:1, half]) / col_stats[1:2, half]
                for i in range(N + 1)
            ]
        total = q[a, *own_block].astype(F32)
        if a == SLOT:
            total = total * scale[N]
        receive(r1.at[a], p1_s.at[a], p1_r.at[a])
        for i in range(N):
            term = r1[a, i].astype(F32)
            total = total + (term * scale[i] if a == SLOT else term)
        hold[a, :, 0:96] = total.T.astype(BF16)
        for i in range(4):
            here = is_primary & owner_self(i)
            owner = (y * 16 + home_z, 2 * (2 * (x // 2) + i // 2) + i % 2)
            part_of = hold.at[a, pl.ds(32 * i, 32)]
            pl.when(jnp.logical_not(here))(
                copy(part_of, coll.at[a, distance], p2_s.at[a], p2_r.at[a, distance], owner).start
            )

            @pl.when(here)
            def _():
                coll[a, 0] = hold[a, 32 * i:32 * i + 32]

        sent.append((copy(coll.at[a, pl.ds(0, 3)], coll.at[a, pl.ds(0, 3)], p2_s.at[a], p2_r.at[a, 0]).wait_send, home_self))
        sent.append((copy(coll.at[a], coll.at[a], p2_s.at[a], p2_r.at[a, 0]).wait_send, jnp.logical_not(home_self)))

    drain(6)
    for a in (BACK, SLOT, GPARAM):
        for g in range(4):
            receive(coll.at[a, g], p2_s.at[a], p2_r.at[a, g], jnp.logical_not(home_self) if g == 0 else None)
        total = coll[a, 0].astype(F32)
        for g in range(1, 4):
            total = total + coll[a, g].astype(F32)
        owned[a] = total.astype(BF16)[:, 0:96]
        stores[a].start()

    for store in stores:
        store.wait()
    drain()


def store_kernel(*refs):
    sources, targets, stages, sem = refs[:5], refs[5:10], refs[10:15], refs[15]
    loads = [pltpu.make_async_copy(a, b, sem.at[0, i]) for i, (a, b) in enumerate(zip(sources, stages))]
    stores = [pltpu.make_async_copy(a, b, sem.at[1, i]) for i, (a, b) in enumerate(zip(stages, targets))]
    for load in loads:
        load.start()
    for load, store in zip(loads, stores):
        load.wait()
        store.start()
    for store in stores:
        store.wait()


def shards(tokens, slot_param, slot_outputs, grad_output, grad_slot_in):
    dma = pltpu.SemaphoreType.DMA
    hbm = pl.BlockSpec(memory_space=pl.ANY)
    out_shape = [
        jax.ShapeDtypeStruct((32, 96), BF16),
        jax.ShapeDtypeStruct((256, 768), BF16),
        jax.ShapeDtypeStruct((256, 768), BF16),
        jax.ShapeDtypeStruct((32, 96), BF16),
        jax.ShapeDtypeStruct((32, 96), BF16),
    ]
    results = pl.pallas_call(
        kernel,
        out_shape=out_shape,
        in_specs=[hbm] * 5,
        out_specs=[hbm] * 5,
        scratch_shapes=[
            pltpu.VMEM((256, 768), BF16),
            pltpu.VMEM((256, 768), BF16),
            pltpu.VMEM((3, 32, 96), BF16),
            pltpu.VMEM((256, 768), BF16),
            pltpu.VMEM((256, 768), BF16),
            pltpu.VMEM((3, 32, 96), BF16),
            pltpu.VMEM((96, 128), BF16),
            pltpu.VMEM((4, 96, 128), BF16),
            pltpu.VMEM((3, 768, 256), BF16),
            pltpu.VMEM((768, 256), BF16),
            pltpu.VMEM((768, 256), BF16),
            pltpu.VMEM((3, 256, 256), F32),
            pltpu.VMEM((3, M, 32, 256), F32),
            pltpu.VMEM((3, 256, 256), F32),
            pltpu.VMEM((M + 1, 2, 256), F32),
            pltpu.VMEM((M + 1, 1, 256), F32),
            pltpu.VMEM((N + 1, 2, 256), F32),
            pltpu.VMEM((N + 1, 1, 256), F32),
            pltpu.VMEM((L + 1, 2, 256), F32),
            pltpu.VMEM((L + 1, 1, 256), F32),
            pltpu.VMEM((2, 256), F32),
            pltpu.VMEM((256, 256), F32),
            pltpu.VMEM((256, 256), F32),
            pltpu.VMEM((256, 256), F32),
            pltpu.VMEM((3, 768, 256), BF16),
            pltpu.VMEM((3, N, 96, 128), BF16),
            pltpu.VMEM((3, 128, 128), BF16),
            pltpu.VMEM((3, 4, 32, 128), BF16),
            dma((5,)), dma((5,)),
            dma, dma((4,)),
            dma((3,)), dma((3,)),
            dma((3,)), dma((3,)),
            dma((3,)), dma((3,)),
            dma((3,)), dma((3,)),
            dma((2,)), dma((2,)),
            dma((2,)), dma((2,)),
            dma((2,)), dma((2,)),
            dma((3,)), dma((3,)),
            dma((3,)), dma((3, 4)),
        ],
        compiler_params=pltpu.CompilerParams(
            collective_id=0, has_side_effects=True, vmem_limit_bytes=60 * 1024 * 1024
        ),
        cost_estimate=pl.CostEstimate(flops=10**9, bytes_accessed=2 * 10**6, transcendentals=10**5),
        name="soft_moe",
    )(tokens, slot_param, slot_outputs, grad_output, grad_slot_in)
    return pl.pallas_call(
        store_kernel,
        out_shape=out_shape,
        in_specs=[hbm] * 5,
        out_specs=[hbm] * 5,
        scratch_shapes=[pltpu.VMEM(o.shape, o.dtype) for o in out_shape] + [dma((2, 5))],
        compiler_params=pltpu.CompilerParams(vmem_limit_bytes=60 * 1024 * 1024),
        name="store_results",
    )(*results)


def solution(mesh):
    by_seq, by_exp = P("seq", "exp"), P("exp", "seq")
    return jax.shard_map(
        shards,
        mesh=mesh,
        in_specs=(by_seq, by_exp, by_exp, by_seq, by_exp),
        out_specs=(by_exp, by_seq, by_seq, by_exp, by_exp),
        check_vma=False,
    )
```

time: 1200 us -> 86.6 us (0.07)
  the two profiles are of different devices: /device:TPU:8 before, /device:TPU:1 now
where the time goes in v2:
time: 86.6 us; the launch traced here: 85.6 us
  Pallas kernels  84.9 us (98%)
    pallas_call x1, Pallas kernels, shards(): pl.pallas_call(kernel, out_shape=out_shape, in_specs=[hbm] * 5, out_specs...  82.9 us
    pallas_call x1, Pallas kernels, shards(): pl.pallas_call(store_kernel, out_shape=out_shape, in_specs=[hbm] * 5, out...  1.98 us

profile of v2, /device:TPU:1, one launch (start us, length us, event | category | flops | bytes accessed | tf_op | source)
XLA Modules:
  0.0 85.6 jit_solution(4542879397380407867)
XLA Ops:
  0.6 82.9 %soft_moe.1 = (bf16[32,96]{1,0:T(8,128)(2,1)}, bf16[256,768]{1,0:T(8,128)(2,1)}, bf16[256,768]{1,0:T(8,128)(2,1)}, bf16[32,96]{1,0:T(8,128)(2,1)}, bf16[32,96]{1,0:T(8,128)(2,1)}) custom-call(bf16[256,768]{1,0:T(8,128)(2,1)} %tok_hbm.1, bf16[32,96]{1,0:T(8,128)(2,1)} %par_hbm.1, bf16[32,96]{1,0:T(8,128)(2,1)} %out_hbm.1, bf16[256,768]{1,0:T(8,128)(2,1)} %go_hbm.1, ...), custom_call_target="tpu_custom_call" | custom-call | flops 1000000000 | bytes 2000000 | tf_op jit(solution)/shard_map/soft_moe/pallas_call | solution.py:414
  83.6 2.0 %store_results.1 = (bf16[32,96]{1,0:T(8,128)(2,1)}, bf16[256,768]{1,0:T(8,128)(2,1)}, bf16[256,768]{1,0:T(8,128)(2,1)}, bf16[32,96]{1,0:T(8,128)(2,1)}, bf16[32,96]{1,0:T(8,128)(2,1)}) custom-call(bf16[32,96]{1,0:T(8,128)(2,1)} %get-tuple-element.10.refs_0_, bf16[256,768]{1,0:T(8,128)(2,1)} %get-tuple-element.11.refs_1_, ...), custom_call_target="tpu_custom_call" | custom-call | tf_op jit(solution)/shard_map/store_results/pallas_call | solution.py:466

commit v3 on v2

--- a/solution.py
+++ b/solution.py
@@ -28,7 +28,7 @@
 def kernel(
     tok_hbm, par_hbm, out_hbm, go_hbm, gsi_hbm,
     slot_in_hbm, layer_hbm, gtok_hbm, gpar_hbm, gso_hbm,
-    layer_ref, gtok_ref, owned, tok, go, small, blk, inbox, w, tok_t, go_t, part, red, full,
+    layer_ref, gtok_ref, owned, tok, go, small, blk, inbox, w, tok_t, go_t, part, red, full, part_b, red_b, full_b,
     grp_m, grp_u, st_m, st_u, far_m, far_u, col_stats, comb, from_combine, disp, q, r1, hold, coll,
     in_sem, out_sem, sp_s, sp_r, wf_s, wf_r, ag_s, ag_r, rs_s, rs_r, eg_s, eg_r,
     gm_s, gm_r, nm_s, nm_r, fm_s, fm_r, p1_s, p1_r, p2_s, p2_r,
@@ -185,28 +185,41 @@
 
     my_tok = pl.multiple_of(32 * e, 32)
 
-    def scatter(a):
+    def parts_of(a):
+        return part if a == PARAM else part_b.at[a - 1]
+
+    def terms_of(a):
+        return red if a == PARAM else red_b.at[a - 1]
+
+    def sums_of(a):
+        return full if a == PARAM else full_b.at[a - 1]
+
+    def scatter(a, product):
+        parts, terms = parts_of(a), terms_of(a)
+        parts[...] = product.astype(parts.dtype)
         copies = []
         for i, o in enumerate(GROUP):
             device = group_id(*o)
-            spot = part.at[a, pl.ds(pl.multiple_of(32 * device[1], 32), 32)]
-            copies.append((spot, red.at[a, i], device))
-        send(copies, red.at[a], rs_s.at[a], rs_r.at[a])
+            spot = parts.at[pl.ds(pl.multiple_of(32 * device[1], 32), 32)]
+            copies.append((spot, terms.at[i], device))
+        send(copies, terms, rs_s.at[a], rs_r.at[a])
 
     def reduced(a):
-        total = part[a, pl.ds(my_tok, 32), :]
-        receive(red.at[a], rs_s.at[a], rs_r.at[a])
+        parts, terms, sums = parts_of(a), terms_of(a), sums_of(a)
+        total = parts[pl.ds(my_tok, 32), :].astype(F32)
+        receive(terms, rs_s.at[a], rs_r.at[a])
         for i in range(M):
-            total = total + red[a, i]
-        full[a, pl.ds(my_tok, 32), :] = total
-        return total
+            total = total + terms[i].astype(F32)
+        total = total.astype(sums.dtype)
+        sums[pl.ds(my_tok, 32), :] = total
+        return total.astype(F32)
 
     def gather(a):
-        spot = full.at[a, pl.ds(my_tok, 32)]
-        send([(spot, spot, group_id(*o)) for o in GROUP], red.at[a], eg_s.at[a], eg_r.at[a])
+        spot = sums_of(a).at[pl.ds(my_tok, 32)]
+        send([(spot, spot, group_id(*o)) for o in GROUP], terms_of(a), eg_s.at[a], eg_r.at[a])
 
     def complete(a):
-        receive(red.at[a], eg_s.at[a], eg_r.at[a])
+        receive(terms_of(a), eg_s.at[a], eg_r.at[a])
 
     def spread(buf, ss, rs, ids, t):
         last = buf.shape[0] - 1
@@ -246,12 +259,8 @@
         send(copies, r1.at[a], p1_s.at[a], p1_r.at[a])
 
     gathered(PARAM)
-    part[PARAM] = dot(tok[...], w[PARAM])
-    scatter(PARAM)
+    scatter(PARAM, dot(tok[...], w[PARAM]))
     pass_on(OUTPUT)
-    gathered(COTAN)
-    part[COTAN] = dot(tok[...], w[COTAN])
-    scatter(COTAN)
 
     own_logits = reduced(PARAM)
     own_max = jnp.max(own_logits, axis=0, keepdims=True)
@@ -260,7 +269,10 @@
     grp_m[M, 1:2] = jnp.sum(own_exp, axis=0, keepdims=True)
     spread(grp_m, gm_s, gm_r, group_ids, 0)
     gather(PARAM)
-    drain(5)
+
+    gathered(COTAN)
+    scatter(COTAN, dot(tok[...], w[COTAN]))
+    drain(4)
 
     arrived(grp_m, gm_s, gm_r, 0)
     group_max, group_total, group_factors = merge(grp_m)
@@ -268,24 +280,20 @@
     st_m[N, 1:2] = group_total
     spread(st_m, nm_s, nm_r, near_ids, 0)
 
+    gathered(OUTPUT)
+    scatter(OUTPUT, dot(go[...], w[OUTPUT]))
+
+    complete(PARAM)
+    logits = full[...]
+    weights = jnp.exp(logits - jnp.max(logits, axis=1, keepdims=True))
+    comb[...] = weights / jnp.sum(weights, axis=1, keepdims=True)
+    partial(BACK, go_t, comb[...].astype(BF16))
+
     own_grad = reduced(COTAN)
     grp_u[M] = jnp.sum(own_exp * own_grad, axis=0, keepdims=True)
     spread(grp_u, gm_s, gm_r, group_ids, 1)
-
-    gathered(OUTPUT)
-    part[OUTPUT] = dot(go[...], w[OUTPUT])
-    scatter(OUTPUT)
     gather(COTAN)
-
-    complete(PARAM)
-    logits = full[PARAM]
-    weights = jnp.exp(logits - jnp.max(logits, axis=1, keepdims=True))
-    comb[...] = weights / jnp.sum(weights, axis=1, keepdims=True)
-    partial(BACK, go_t, comb[...].astype(BF16))
-
-    arrived(grp_u, gm_s, gm_r, 1)
-    st_u[N] = merge_inner(grp_u, group_factors)
-    spread(st_u, nm_s, nm_r, near_ids, 1)
+    partial(SLOT, tok_t, jnp.exp(full[...] - group_max).astype(BF16))
 
     arrived(st_m, nm_s, nm_r, 0)
     near_max, near_total, near_factors = merge(st_m)
@@ -294,38 +302,38 @@
     spread(far_m, fm_s, fm_r, far_ids, 0)
     partial_out(BACK)
 
-    partial(SLOT, tok_t, jnp.exp(full[PARAM] - group_max).astype(BF16))
-    drain(4)
-
     reduced(OUTPUT)
     gather(OUTPUT)
+
+    arrived(grp_u, gm_s, gm_r, 1)
+    group_inner = merge_inner(grp_u, group_factors)
+    st_u[N] = group_inner
+    spread(st_u, nm_s, nm_r, near_ids, 1)
+    partial_out(SLOT)
+    drain(6)
+
+    complete(COTAN)
+    complete(OUTPUT)
+    combine_full = comb[...]
+    grad_combine = full_b[OUTPUT - 1].astype(F32)
+    from_combine[...] = combine_full * (
+        grad_combine - jnp.sum(combine_full * grad_combine, axis=1, keepdims=True)
+    )
 
     arrived(st_u, nm_s, nm_r, 1)
     far_u[L] = merge_inner(st_u, near_factors)
     spread(far_u, fm_s, fm_r, far_ids, 1)
-    partial_out(SLOT)
-
-    complete(COTAN)
-    complete(OUTPUT)
-    combine_full = comb[...]
-    grad_combine = full[OUTPUT]
-    from_combine[...] = combine_full * (
-        grad_combine - jnp.sum(combine_full * grad_combine, axis=1, keepdims=True)
-    )
 
     arrived(far_m, fm_s, fm_r, 0)
     col_max, col_total, far_factors = merge(far_m)
     col_stats[0:1] = col_max
     col_stats[1:2] = col_total
-    disp[...] = jnp.exp(full[PARAM] - col_max) / col_total
-    drain(2)
-
-    arrived(far_u, fm_s, fm_r, 1)
-    inner = merge_inner(far_u, far_factors) / col_total
-    grad_logits = (from_combine[...] + disp[...] * (full[COTAN] - inner)).astype(BF16)
-    partial(GPARAM, tok_t, grad_logits)
+    disp[...] = jnp.exp(full[...] - col_max) / col_total
+
+    centre = group_inner / group_total
+    grad_dispatch = full_b[COTAN - 1].astype(F32)
+    partial(GPARAM, tok_t, (from_combine[...] + disp[...] * (grad_dispatch - centre)).astype(BF16))
     partial_out(GPARAM)
-
     stores = [
         pltpu.make_async_copy(src, dst, out_sem.at[i])
         for i, (src, dst) in enumerate((
@@ -335,21 +343,28 @@
     ]
     layer_ref[...] = rows_by_rows(comb[...].astype(BF16), w[OUTPUT]).astype(BF16)
     stores[3].start()
-    gtok_ref[...] = (
-        rows_by_rows(disp[...].astype(BF16), w[COTAN]) + rows_by_rows(grad_logits, w[PARAM])
-    ).astype(BF16)
-    stores[4].start()
 
     distance = (z // 4 - 2 * c - x % 2 + 4) % 4
     home_z = 8 * c + 4 * (x % 2) + z % 4
     hold[...] = jnp.zeros_like(hold)
+    half = own_block[1]
     for a in (BACK, SLOT, GPARAM):
         if a == SLOT:
-            half = own_block[1]
             scale = [
                 jnp.exp(st_m[i, 0:1, half] - col_stats[0:1, half]) / col_stats[1:2, half]
                 for i in range(N + 1)
             ]
+        if a == GPARAM:
+            arrived(far_u, fm_s, fm_r, 1)
+            inner = merge_inner(far_u, far_factors) / col_total
+            col_stats[2:3] = inner
+            grad_logits = (
+                from_combine[...] + disp[...] * (full_b[COTAN - 1].astype(F32) - inner)
+            ).astype(BF16)
+            gtok_ref[...] = (
+                rows_by_rows(disp[...].astype(BF16), w[COTAN]) + rows_by_rows(grad_logits, w[PARAM])
+            ).astype(BF16)
+            stores[4].start()
         total = q[a, *own_block].astype(F32)
         if a == SLOT:
             total = total * scale[N]
@@ -357,6 +372,11 @@
         for i in range(N):
             term = r1[a, i].astype(F32)
             total = total + (term * scale[i] if a == SLOT else term)
+        if a == GPARAM:
+            for i in range(N + 1):
+                shift = (st_u[i, 0:1, half] / st_m[i, 1:2, half] - col_stats[2:3, half]) * scale[i]
+                term = r1[SLOT, i] if i < N else q[SLOT, *own_block]
+                total = total + term.astype(F32) * shift
         hold[a, :, 0:96] = total.T.astype(BF16)
         for i in range(4):
             here = is_primary & owner_self(i)
@@ -428,16 +448,19 @@
             pltpu.VMEM((3, 768, 256), BF16),
             pltpu.VMEM((768, 256), BF16),
             pltpu.VMEM((768, 256), BF16),
-            pltpu.VMEM((3, 256, 256), F32),
-            pltpu.VMEM((3, M, 32, 256), F32),
-            pltpu.VMEM((3, 256, 256), F32),
+            pltpu.VMEM((256, 256), F32),
+            pltpu.VMEM((M, 32, 256), F32),
+            pltpu.VMEM((256, 256), F32),
+            pltpu.VMEM((2, 256, 256), BF16),
+            pltpu.VMEM((2, M, 32, 256), BF16),
+            pltpu.VMEM((2, 256, 256), BF16),
             pltpu.VMEM((M + 1, 2, 256), F32),
             pltpu.VMEM((M + 1, 1, 256), F32),
             pltpu.VMEM((N + 1, 2, 256), F32),
             pltpu.VMEM((N + 1, 1, 256), F32),
             pltpu.VMEM((L + 1, 2, 256), F32),
             pltpu.VMEM((L + 1, 1, 256), F32),
-            pltpu.VMEM((2, 256), F32),
+            pltpu.VMEM((3, 256), F32),
             pltpu.VMEM((256, 256), F32),
             pltpu.VMEM((256, 256), F32),
             pltpu.VMEM((256, 256), F32),

time: 86.6 us -> 83 us (0.958)
  the two profiles are of different devices: /device:TPU:1 before, /device:TPU:7 now
where the time goes in v3:
time: 83 us; the launch traced here: 82.7 us
  Pallas kernels  82.1 us (99%)
    pallas_call x1, Pallas kernels, shards(): pl.pallas_call(kernel, out_shape=out_shape, in_specs=[hbm] * 5, out_specs...  80.1 us
    pallas_call x1, Pallas kernels, shards(): pl.pallas_call(store_kernel, out_shape=out_shape, in_specs=[hbm] * 5, out...  1.98 us

profile of v3, /device:TPU:7, one launch (start us, length us, event | category | flops | bytes accessed | tf_op | source)
XLA Modules:
  0.0 82.7 jit_solution(16031113581444767593)
XLA Ops:
  0.6 80.1 %soft_moe.1 = (bf16[32,96]{1,0:T(8,128)(2,1)}, bf16[256,768]{1,0:T(8,128)(2,1)}, bf16[256,768]{1,0:T(8,128)(2,1)}, bf16[32,96]{1,0:T(8,128)(2,1)}, bf16[32,96]{1,0:T(8,128)(2,1)}) custom-call(bf16[256,768]{1,0:T(8,128)(2,1)} %tok_hbm.1, bf16[32,96]{1,0:T(8,128)(2,1)} %par_hbm.1, bf16[32,96]{1,0:T(8,128)(2,1)} %out_hbm.1, bf16[256,768]{1,0:T(8,128)(2,1)} %go_hbm.1, ...), custom_call_target="tpu_custom_call" | custom-call | flops 1000000000 | bytes 2000000 | tf_op jit(solution)/shard_map/soft_moe/pallas_call | solution.py:434
  80.7 2.0 %store_results.1 = (bf16[32,96]{1,0:T(8,128)(2,1)}, bf16[256,768]{1,0:T(8,128)(2,1)}, bf16[256,768]{1,0:T(8,128)(2,1)}, bf16[32,96]{1,0:T(8,128)(2,1)}, bf16[32,96]{1,0:T(8,128)(2,1)}) custom-call(bf16[32,96]{1,0:T(8,128)(2,1)} %get-tuple-element.10.refs_0_, bf16[256,768]{1,0:T(8,128)(2,1)} %get-tuple-element.11.refs_1_, ...), custom_call_target="tpu_custom_call" | custom-call | tf_op jit(solution)/shard_map/store_results/pallas_call | solution.py:489

commit v4 on v3

--- a/solution.py
+++ b/solution.py
@@ -30,7 +30,7 @@
     slot_in_hbm, layer_hbm, gtok_hbm, gpar_hbm, gso_hbm,
     layer_ref, gtok_ref, owned, tok, go, small, blk, inbox, w, tok_t, go_t, part, red, full, part_b, red_b, full_b,
     grp_m, grp_u, st_m, st_u, far_m, far_u, col_stats, comb, from_combine, disp, q, r1, hold, coll,
-    in_sem, out_sem, sp_s, sp_r, wf_s, wf_r, ag_s, ag_r, rs_s, rs_r, eg_s, eg_r,
+    in_sem, out_sem, sp_s, sp_r, wf_s, wf_r, ag_s, ag_r, ah_s, ah_r, rs_s, rs_r, eg_s, eg_r,
     gm_s, gm_r, nm_s, nm_r, fm_s, fm_r, p1_s, p1_r, p2_s, p2_r,
 ):
     s, e = lax.axis_index("seq"), lax.axis_index("exp")
@@ -66,24 +66,32 @@
     def group_id(dy, dc):
         return (s, ((y + dy) % 4) * 2 + (c + dc) % 2)
 
+    def share_of(bx):
+        u = (bx - y + 4) % 4
+        return ((u + 1) // 2) % 2, (y // 2 + 1 + u // 2) % 2
+
+    h_own, s_own = share_of(x)
+
     def block_of(bx, bz):
-        row = pl.multiple_of(96 * (4 * (bx % 2) + bz % 4), 32)
-        col = pl.multiple_of(128 * (bx // 2), 128)
-        return pl.ds(row, 96), pl.ds(col, 128)
+        h, half = share_of(bx)
+        row = pl.multiple_of(96 * (4 * h + bz % 4), 32)
+        return pl.ds(row, 96), pl.ds(pl.multiple_of(128 * half, 128), 128)
 
     own_block = block_of(x, z)
-    is_primary = z // 4 == 2 * c + x % 2
+    is_primary = z // 4 == 2 * c + h_own
     not_primary = jnp.logical_not(is_primary)
-    primary_id = (x * 16 + 8 * c + 4 * (x % 2) + z % 4, e)
-    home_id = ((2 * (y // 2) + (z % 8) // 4) * 16 + z, 2 * x + z // 8)
-    home_self = (x == y) & is_primary
+    h_home = (z % 8) // 4
+    same_half = 1 - (y // 2 + x // 2) % 2
+    home_x = (x + h_home + same_half * (3 - 2 * h_home)) % 4
+    home_id = (home_x * 16 + z, 2 * x + z // 8)
+    home_self = (home_x == x) & (x == y) & (c == z // 8)
     place = 2 * (y % 2) + c
 
     def owner_id(i):
-        return (y * 16 + z, 2 * (2 * (x // 2) + i // 2) + i % 2)
+        return (y * 16 + z, 2 * (2 * s_own + i // 2) + i % 2)
 
     def owner_self(i):
-        return (x == y) & (y == 2 * (x // 2) + i // 2) & (c == i % 2)
+        return (x == y) & (y == 2 * s_own + i // 2) & (c == i % 2)
 
     barrier = pltpu.get_barrier_semaphore()
 
@@ -161,10 +169,26 @@
         for i in range(4):
             receive(inbox.at[i], sp_s, sp_r.at[i], jnp.logical_not(owner_self(i)))
 
+    def first_peers(a):
+        if a == PARAM:
+            return NEAR
+        return [o for o in NEAR if o[a - 1] == 0]
+
     def pass_on(a):
         spot = w.at[a, *own_block]
         receive(spot, wf_s.at[a], wf_r.at[a], not_primary)
-        send([(spot, spot, near_id(*o)) for o in NEAR], r1.at[a], ag_s.at[a], ag_r.at[a])
+        peers = first_peers(a)
+        send([(spot, spot, near_id(*o)) for o in peers], r1.at[a, pl.ds(0, len(peers))], ag_s.at[a], ag_r.at[a])
+
+    def pass_along(a):
+        receive(r1.at[a, pl.ds(0, 3)], ag_s.at[a], ag_r.at[a])
+        if a == COTAN:
+            row, col = pl.multiple_of(384 * h_own, 128), pl.multiple_of(128 * s_own, 128)
+            spots = [w.at[a, pl.ds(row, 384), pl.ds(col, 128)]]
+        else:
+            spots = [w.at[a, pl.ds(pl.multiple_of(96 * (4 * h + z % 4), 32), 96)] for h in (0, 1)]
+        peers = [near_id(*o) for o in NEAR if o[2 - a] == 0]
+        send([(spot, spot, p) for p in peers for spot in spots], w.at[a, pl.ds(0, 576)], ah_s.at[a - 1], ah_r.at[a - 1])
 
     for a in (PARAM, COTAN, OUTPUT):
         spot = w.at[a, *own_block]
@@ -177,11 +201,13 @@
         send(
             [(spot, spot, far_id(dz)) for dz in FAR], r1.at[a, pl.ds(0, L)], wf_s.at[a], wf_r.at[a], is_primary
         )
-        if a != OUTPUT:
-            pass_on(a)
+        pass_on(a)
 
     def gathered(a):
-        receive(r1.at[a], ag_s.at[a], ag_r.at[a])
+        if a == PARAM:
+            receive(r1.at[a], ag_s.at[a], ag_r.at[a])
+        else:
+            receive(w.at[a, pl.ds(0, 576)], ah_s.at[a - 1], ah_r.at[a - 1])
 
     my_tok = pl.multiple_of(32 * e, 32)
 
@@ -216,10 +242,10 @@
 
     def gather(a):
         spot = sums_of(a).at[pl.ds(my_tok, 32)]
-        send([(spot, spot, group_id(*o)) for o in GROUP], terms_of(a), eg_s.at[a], eg_r.at[a])
+        send([(spot, spot, group_id(*o)) for o in GROUP], red, eg_s.at[a], eg_r.at[a])
 
     def complete(a):
-        receive(terms_of(a), eg_s.at[a], eg_r.at[a])
+        receive(red, eg_s.at[a], eg_r.at[a])
 
     def spread(buf, ss, rs, ids, t):
         last = buf.shape[0] - 1
@@ -260,7 +286,8 @@
 
     gathered(PARAM)
     scatter(PARAM, dot(tok[...], w[PARAM]))
-    pass_on(OUTPUT)
+    pass_along(COTAN)
+    pass_along(OUTPUT)
 
     own_logits = reduced(PARAM)
     own_max = jnp.max(own_logits, axis=0, keepdims=True)
@@ -288,6 +315,7 @@
     weights = jnp.exp(logits - jnp.max(logits, axis=1, keepdims=True))
     comb[...] = weights / jnp.sum(weights, axis=1, keepdims=True)
     partial(BACK, go_t, comb[...].astype(BF16))
+    partial_out(BACK)
 
     own_grad = reduced(COTAN)
     grp_u[M] = jnp.sum(own_exp * own_grad, axis=0, keepdims=True)
@@ -300,7 +328,6 @@
     far_m[L, 0:1] = near_max
     far_m[L, 1:2] = near_total
     spread(far_m, fm_s, fm_r, far_ids, 0)
-    partial_out(BACK)
 
     reduced(OUTPUT)
     gather(OUTPUT)
@@ -320,10 +347,6 @@
         grad_combine - jnp.sum(combine_full * grad_combine, axis=1, keepdims=True)
     )
 
-    arrived(st_u, nm_s, nm_r, 1)
-    far_u[L] = merge_inner(st_u, near_factors)
-    spread(far_u, fm_s, fm_r, far_ids, 1)
-
     arrived(far_m, fm_s, fm_r, 0)
     col_max, col_total, far_factors = merge(far_m)
     col_stats[0:1] = col_max
@@ -333,6 +356,9 @@
     centre = group_inner / group_total
     grad_dispatch = full_b[COTAN - 1].astype(F32)
     partial(GPARAM, tok_t, (from_combine[...] + disp[...] * (grad_dispatch - centre)).astype(BF16))
+    arrived(st_u, nm_s, nm_r, 1)
+    far_u[L] = merge_inner(st_u, near_factors)
+    spread(far_u, fm_s, fm_r, far_ids, 1)
     partial_out(GPARAM)
     stores = [
         pltpu.make_async_copy(src, dst, out_sem.at[i])
@@ -344,8 +370,8 @@
     layer_ref[...] = rows_by_rows(comb[...].astype(BF16), w[OUTPUT]).astype(BF16)
     stores[3].start()
 
-    distance = (z // 4 - 2 * c - x % 2 + 4) % 4
-    home_z = 8 * c + 4 * (x % 2) + z % 4
+    distance = (z // 4 - 2 * c - h_own + 4) % 4
+    home_z = 8 * c + 4 * h_own + z % 4
     hold[...] = jnp.zeros_like(hold)
     half = own_block[1]
     for a in (BACK, SLOT, GPARAM):
@@ -368,19 +394,19 @@
         total = q[a, *own_block].astype(F32)
         if a == SLOT:
             total = total * scale[N]
-        receive(r1.at[a], p1_s.at[a], p1_r.at[a])
-        for i in range(N):
-            term = r1[a, i].astype(F32)
-            total = total + (term * scale[i] if a == SLOT else term)
         if a == GPARAM:
             for i in range(N + 1):
                 shift = (st_u[i, 0:1, half] / st_m[i, 1:2, half] - col_stats[2:3, half]) * scale[i]
                 term = r1[SLOT, i] if i < N else q[SLOT, *own_block]
                 total = total + term.astype(F32) * shift
+        receive(r1.at[a], p1_s.at[a], p1_r.at[a])
+        for i in range(N):
+            term = r1[a, i].astype(F32)
+            total = total + (term * scale[i] if a == SLOT else term)
         hold[a, :, 0:96] = total.T.astype(BF16)
         for i in range(4):
             here = is_primary & owner_self(i)
-            owner = (y * 16 + home_z, 2 * (2 * (x // 2) + i // 2) + i % 2)
+            owner = (y * 16 + home_z, 2 * (2 * s_own + i // 2) + i % 2)
             part_of = hold.at[a, pl.ds(32 * i, 32)]
             pl.when(jnp.logical_not(here))(
                 copy(part_of, coll.at[a, distance], p2_s.at[a], p2_r.at[a, distance], owner).start
@@ -453,7 +479,7 @@
             pltpu.VMEM((256, 256), F32),
             pltpu.VMEM((2, 256, 256), BF16),
             pltpu.VMEM((2, M, 32, 256), BF16),
-            pltpu.VMEM((2, 256, 256), BF16),
+            pltpu.VMEM((2, 256, 256), F32),
             pltpu.VMEM((M + 1, 2, 256), F32),
             pltpu.VMEM((M + 1, 1, 256), F32),
             pltpu.VMEM((N + 1, 2, 256), F32),
@@ -472,6 +498,7 @@
             dma, dma((4,)),
             dma((3,)), dma((3,)),
             dma((3,)), dma((3,)),
+            dma((2,)), dma((2,)),
             dma((3,)), dma((3,)),
             dma((3,)), dma((3,)),
             dma((2,)), dma((2,)),

time: 83 us -> 81.6 us (0.983)
  the two profiles are of different devices: /device:TPU:7 before, /device:TPU:1 now
where the time goes in v4:
time: 81.6 us; the launch traced here: 81.4 us
  Pallas kernels  80.7 us (99%)
    pallas_call x1, Pallas kernels, shards(): pl.pallas_call(kernel, out_shape=out_shape, in_specs=[hbm] * 5, out_specs...  78.7 us
    pallas_call x1, Pallas kernels, shards(): pl.pallas_call(store_kernel, out_shape=out_shape, in_specs=[hbm] * 5, out...  1.98 us

profile of v4, /device:TPU:1, one launch (start us, length us, event | category | flops | bytes accessed | tf_op | source)
XLA Modules:
  0.0 81.4 jit_solution(17146598428701310348)
XLA Ops:
  0.6 78.7 %soft_moe.1 = (bf16[32,96]{1,0:T(8,128)(2,1)}, bf16[256,768]{1,0:T(8,128)(2,1)}, bf16[256,768]{1,0:T(8,128)(2,1)}, bf16[32,96]{1,0:T(8,128)(2,1)}, bf16[32,96]{1,0:T(8,128)(2,1)}) custom-call(bf16[256,768]{1,0:T(8,128)(2,1)} %tok_hbm.1, bf16[32,96]{1,0:T(8,128)(2,1)} %par_hbm.1, bf16[32,96]{1,0:T(8,128)(2,1)} %out_hbm.1, bf16[256,768]{1,0:T(8,128)(2,1)} %go_hbm.1, ...), custom_call_target="tpu_custom_call" | custom-call | flops 1000000000 | bytes 2000000 | tf_op jit(solution)/shard_map/soft_moe/pallas_call | solution.py:460
  79.4 2.0 %store_results.1 = (bf16[32,96]{1,0:T(8,128)(2,1)}, bf16[256,768]{1,0:T(8,128)(2,1)}, bf16[256,768]{1,0:T(8,128)(2,1)}, bf16[32,96]{1,0:T(8,128)(2,1)}, bf16[32,96]{1,0:T(8,128)(2,1)}) custom-call(bf16[32,96]{1,0:T(8,128)(2,1)} %get-tuple-element.10.refs_0_, bf16[256,768]{1,0:T(8,128)(2,1)} %get-tuple-element.11.refs_1_, ...), custom_call_target="tpu_custom_call" | custom-call | tf_op jit(solution)/shard_map/store_results/pallas_call | solution.py:516

commit v5 on v4

--- a/solution.py
+++ b/solution.py
@@ -13,6 +13,9 @@
 FAR = [8, 4, -4]
 GROUP = [(dy, dc) for dy in (2, 1, 3, 0) for dc in (1, 0) if (dy, dc) != (0, 0)]
 N, M, L = len(NEAR), len(GROUP), len(FAR)
+PLANE = [(dx, dy, dc) for dx in (2, 1, 3, 0) for dy in (2, 1, 3, 0) for dc in (1, 0) if (dx, dy, dc) != (0, 0, 0)]
+LINE = [8, 7, -7, 6, -6, 5, -5, 4, -4, 3, -3, 2, -2, 1, -1]
+A, B = len(PLANE), len(LINE)
 PARAM, COTAN, OUTPUT = 0, 1, 2
 BACK, SLOT, GPARAM = 0, 1, 2
 
@@ -29,9 +32,9 @@
     tok_hbm, par_hbm, out_hbm, go_hbm, gsi_hbm,
     slot_in_hbm, layer_hbm, gtok_hbm, gpar_hbm, gso_hbm,
     layer_ref, gtok_ref, owned, tok, go, small, blk, inbox, w, tok_t, go_t, part, red, full, part_b, red_b, full_b,
-    grp_m, grp_u, st_m, st_u, far_m, far_u, col_stats, comb, from_combine, disp, q, r1, hold, coll,
+    pl_m, pl_u, ln_m, ln_u, cen, col_stats, comb, from_combine, disp, expo, q, r1, hold, coll,
     in_sem, out_sem, sp_s, sp_r, wf_s, wf_r, ag_s, ag_r, ah_s, ah_r, rs_s, rs_r, eg_s, eg_r,
-    gm_s, gm_r, nm_s, nm_r, fm_s, fm_r, p1_s, p1_r, p2_s, p2_r,
+    pm_s, pm_r, lm_s, lm_r, cn_s, cn_r, p1_s, p1_r, p2_s, p2_r,
 ):
     s, e = lax.axis_index("seq"), lax.axis_index("exp")
     x, z = s // 16, s % 16
@@ -242,10 +245,10 @@
 
     def gather(a):
         spot = sums_of(a).at[pl.ds(my_tok, 32)]
-        send([(spot, spot, group_id(*o)) for o in GROUP], red, eg_s.at[a], eg_r.at[a])
+        send([(spot, spot, group_id(*o)) for o in GROUP], terms_of(a), eg_s.at[a], eg_r.at[a])
 
     def complete(a):
-        receive(red, eg_s.at[a], eg_r.at[a])
+        receive(terms_of(a), eg_s.at[a], eg_r.at[a])
 
     def spread(buf, ss, rs, ids, t):
         last = buf.shape[0] - 1
@@ -272,9 +275,11 @@
             total = total + factors[i] * buf[i]
         return total
 
-    group_ids = [group_id(*o) for o in GROUP]
+    plane_ids = [
+        (((x + dx) % 4) * 16 + z, ((y + dy) % 4) * 2 + (c + dc) % 2) for dx, dy, dc in PLANE
+    ]
+    line_ids = [far_id(dz) for dz in LINE]
     near_ids = [near_id(*o) for o in NEAR]
-    far_ids = [far_id(dz) for dz in FAR]
 
     def partial(a, left_t, right):
         for r in range(3):
@@ -292,20 +297,20 @@
     own_logits = reduced(PARAM)
     own_max = jnp.max(own_logits, axis=0, keepdims=True)
     own_exp = jnp.exp(own_logits - own_max)
-    grp_m[M, 0:1] = own_max
-    grp_m[M, 1:2] = jnp.sum(own_exp, axis=0, keepdims=True)
-    spread(grp_m, gm_s, gm_r, group_ids, 0)
+    pl_m[A, 0:1] = own_max
+    pl_m[A, 1:2] = jnp.sum(own_exp, axis=0, keepdims=True)
+    spread(pl_m, pm_s, pm_r, plane_ids, 0)
     gather(PARAM)
 
     gathered(COTAN)
     scatter(COTAN, dot(tok[...], w[COTAN]))
     drain(4)
 
-    arrived(grp_m, gm_s, gm_r, 0)
-    group_max, group_total, group_factors = merge(grp_m)
-    st_m[N, 0:1] = group_max
-    st_m[N, 1:2] = group_total
-    spread(st_m, nm_s, nm_r, near_ids, 0)
+    arrived(pl_m, pm_s, pm_r, 0)
+    plane_max, plane_total, plane_factors = merge(pl_m)
+    ln_m[B, 0:1] = plane_max
+    ln_m[B, 1:2] = plane_total
+    spread(ln_m, lm_s, lm_r, line_ids, 0)
 
     gathered(OUTPUT)
     scatter(OUTPUT, dot(go[...], w[OUTPUT]))
@@ -318,28 +323,23 @@
     partial_out(BACK)
 
     own_grad = reduced(COTAN)
-    grp_u[M] = jnp.sum(own_exp * own_grad, axis=0, keepdims=True)
-    spread(grp_u, gm_s, gm_r, group_ids, 1)
+    pl_u[A] = jnp.sum(own_exp * own_grad, axis=0, keepdims=True)
+    spread(pl_u, pm_s, pm_r, plane_ids, 1)
     gather(COTAN)
-    partial(SLOT, tok_t, jnp.exp(full[...] - group_max).astype(BF16))
-
-    arrived(st_m, nm_s, nm_r, 0)
-    near_max, near_total, near_factors = merge(st_m)
-    far_m[L, 0:1] = near_max
-    far_m[L, 1:2] = near_total
-    spread(far_m, fm_s, fm_r, far_ids, 0)
+    expo[...] = jnp.exp(full[...] - plane_max)
+    partial(SLOT, tok_t, expo[...].astype(BF16))
+    partial_out(SLOT)
 
     reduced(OUTPUT)
     gather(OUTPUT)
 
-    arrived(grp_u, gm_s, gm_r, 1)
-    group_inner = merge_inner(grp_u, group_factors)
-    st_u[N] = group_inner
-    spread(st_u, nm_s, nm_r, near_ids, 1)
-    partial_out(SLOT)
-    drain(6)
-
     complete(COTAN)
+    centre = jnp.sum(expo[...] * full_b[COTAN - 1].astype(F32), axis=0, keepdims=True) / (
+        jnp.maximum(jnp.sum(expo[...], axis=0, keepdims=True), 1e-30)
+    )
+    cen[N] = centre
+    spread(cen, cn_s, cn_r, near_ids, 0)
+
     complete(OUTPUT)
     combine_full = comb[...]
     grad_combine = full_b[OUTPUT - 1].astype(F32)
@@ -347,19 +347,20 @@
         grad_combine - jnp.sum(combine_full * grad_combine, axis=1, keepdims=True)
     )
 
-    arrived(far_m, fm_s, fm_r, 0)
-    col_max, col_total, far_factors = merge(far_m)
+    arrived(ln_m, lm_s, lm_r, 0)
+    col_max, col_total, line_factors = merge(ln_m)
     col_stats[0:1] = col_max
     col_stats[1:2] = col_total
     disp[...] = jnp.exp(full[...] - col_max) / col_total
-
-    centre = group_inner / group_total
     grad_dispatch = full_b[COTAN - 1].astype(F32)
     partial(GPARAM, tok_t, (from_combine[...] + disp[...] * (grad_dispatch - centre)).astype(BF16))
-    arrived(st_u, nm_s, nm_r, 1)
-    far_u[L] = merge_inner(st_u, near_factors)
-    spread(far_u, fm_s, fm_r, far_ids, 1)
+
+    arrived(pl_u, pm_s, pm_r, 1)
+    ln_u[B] = merge_inner(pl_u, plane_factors)
+    spread(ln_u, lm_s, lm_r, line_ids, 1)
     partial_out(GPARAM)
+    drain(6)
+
     stores = [
         pltpu.make_async_copy(src, dst, out_sem.at[i])
         for i, (src, dst) in enumerate((
@@ -375,34 +376,31 @@
     hold[...] = jnp.zeros_like(hold)
     half = own_block[1]
     for a in (BACK, SLOT, GPARAM):
+        if a == GPARAM:
+            arrived(ln_u, lm_s, lm_r, 1)
+            inner = merge_inner(ln_u, line_factors) / col_total
+            col_stats[2:3] = inner
+        total = q[a, *own_block].astype(F32)
+        receive(r1.at[a], p1_s.at[a], p1_r.at[a])
         if a == SLOT:
-            scale = [
-                jnp.exp(st_m[i, 0:1, half] - col_stats[0:1, half]) / col_stats[1:2, half]
-                for i in range(N + 1)
-            ]
+            arrived(cen, cn_s, cn_r, 0)
+            at_z = {0: B, 1: LINE.index(1), -1: LINE.index(-1), 2: jnp.where(c == 0, LINE.index(2), LINE.index(-2))}
+            scale = {
+                dz: jnp.exp(ln_m[i, 0:1, half] - col_stats[0:1, half]) / col_stats[1:2, half]
+                for dz, i in at_z.items()
+            }
+            total = total * scale[0]
+            centred = total * cen[N, 0:1, half]
+            for i, (dx, dz) in enumerate(NEAR):
+                term = r1[SLOT, i].astype(F32) * scale[dz]
+                total = total + term
+                centred = centred + term * cen[i, 0:1, half]
+            slot_total = total
+        else:
+            for i in range(N):
+                total = total + r1[a, i].astype(F32)
         if a == GPARAM:
-            arrived(far_u, fm_s, fm_r, 1)
-            inner = merge_inner(far_u, far_factors) / col_total
-            col_stats[2:3] = inner
-            grad_logits = (
-                from_combine[...] + disp[...] * (full_b[COTAN - 1].astype(F32) - inner)
-            ).astype(BF16)
-            gtok_ref[...] = (
-                rows_by_rows(disp[...].astype(BF16), w[COTAN]) + rows_by_rows(grad_logits, w[PARAM])
-            ).astype(BF16)
-            stores[4].start()
-        total = q[a, *own_block].astype(F32)
-        if a == SLOT:
-            total = total * scale[N]
-        if a == GPARAM:
-            for i in range(N + 1):
-                shift = (st_u[i, 0:1, half] / st_m[i, 1:2, half] - col_stats[2:3, half]) * scale[i]
-                term = r1[SLOT, i] if i < N else q[SLOT, *own_block]
-                total = total + term.astype(F32) * shift
-        receive(r1.at[a], p1_s.at[a], p1_r.at[a])
-        for i in range(N):
-            term = r1[a, i].astype(F32)
-            total = total + (term * scale[i] if a == SLOT else term)
+            total = total + centred - slot_total * col_stats[2:3, half]
         hold[a, :, 0:96] = total.T.astype(BF16)
         for i in range(4):
             here = is_primary & owner_self(i)
@@ -419,6 +417,11 @@
         sent.append((copy(coll.at[a, pl.ds(0, 3)], coll.at[a, pl.ds(0, 3)], p2_s.at[a], p2_r.at[a, 0]).wait_send, home_self))
         sent.append((copy(coll.at[a], coll.at[a], p2_s.at[a], p2_r.at[a, 0]).wait_send, jnp.logical_not(home_self)))
 
+    grad_logits = (from_combine[...] + disp[...] * (full_b[COTAN - 1].astype(F32) - col_stats[2:3])).astype(BF16)
+    gtok_ref[...] = (
+        rows_by_rows(disp[...].astype(BF16), w[COTAN]) + rows_by_rows(grad_logits, w[PARAM])
+    ).astype(BF16)
+    stores[4].start()
     drain(6)
     for a in (BACK, SLOT, GPARAM):
         for g in range(4):
@@ -479,14 +482,14 @@
             pltpu.VMEM((256, 256), F32),
             pltpu.VMEM((2, 256, 256), BF16),
             pltpu.VMEM((2, M, 32, 256), BF16),
-            pltpu.VMEM((2, 256, 256), F32),
-            pltpu.VMEM((M + 1, 2, 256), F32),
-            pltpu.VMEM((M + 1, 1, 256), F32),
-            pltpu.VMEM((N + 1, 2, 256), F32),
+            pltpu.VMEM((2, 256, 256), BF16),
+            pltpu.VMEM((A + 1, 2, 256), F32),
+            pltpu.VMEM((A + 1, 1, 256), F32),
+            pltpu.VMEM((B + 1, 2, 256), F32),
+            pltpu.VMEM((B + 1, 1, 256), F32),
             pltpu.VMEM((N + 1, 1, 256), F32),
-            pltpu.VMEM((L + 1, 2, 256), F32),
-            pltpu.VMEM((L + 1, 1, 256), F32),
             pltpu.VMEM((3, 256), F32),
+            pltpu.VMEM((256, 256), F32),
             pltpu.VMEM((256, 256), F32),
             pltpu.VMEM((256, 256), F32),
             pltpu.VMEM((256, 256), F32),
@@ -503,7 +506,7 @@
             dma((3,)), dma((3,)),
             dma((2,)), dma((2,)),
             dma((2,)), dma((2,)),
-            dma((2,)), dma((2,)),
+            dma((1,)), dma((1,)),
             dma((3,)), dma((3,)),
             dma((3,)), dma((3, 4)),
         ],

time: 81.6 us -> 80.8 us (level)
    pallas_call x1, Pallas kernels: 78.7 us -> 77.9 us  [shards(): pl.pallas_call(kernel, out_shape=out_shape, in_specs=[hbm] * 5, out_specs...]
where the time goes in v5:
time: 80.8 us; the launch traced here: 80.5 us
  Pallas kernels  79.9 us (99%)
    pallas_call x1, Pallas kernels, shards(): pl.pallas_call(kernel, out_shape=out_shape, in_specs=[hbm] * 5, out_specs...  77.9 us
    pallas_call x1, Pallas kernels, shards(): pl.pallas_call(store_kernel, out_shape=out_shape, in_specs=[hbm] * 5, out...  1.98 us

profile of v5, /device:TPU:1, one launch (start us, length us, event | category | flops | bytes accessed | tf_op | source)
XLA Modules:
  0.0 80.5 jit_solution(5223872283436439948)
XLA Ops:
  0.6 77.9 %soft_moe.1 = (bf16[32,96]{1,0:T(8,128)(2,1)}, bf16[256,768]{1,0:T(8,128)(2,1)}, bf16[256,768]{1,0:T(8,128)(2,1)}, bf16[32,96]{1,0:T(8,128)(2,1)}, bf16[32,96]{1,0:T(8,128)(2,1)}) custom-call(bf16[256,768]{1,0:T(8,128)(2,1)} %tok_hbm.1, bf16[32,96]{1,0:T(8,128)(2,1)} %par_hbm.1, bf16[32,96]{1,0:T(8,128)(2,1)} %out_hbm.1, bf16[256,768]{1,0:T(8,128)(2,1)} %go_hbm.1, ...), custom_call_target="tpu_custom_call" | custom-call | flops 1000000000 | bytes 2000000 | tf_op jit(solution)/shard_map/soft_moe/pallas_call | solution.py:463
  78.5 2.0 %store_results.1 = (bf16[32,96]{1,0:T(8,128)(2,1)}, bf16[256,768]{1,0:T(8,128)(2,1)}, bf16[256,768]{1,0:T(8,128)(2,1)}, bf16[32,96]{1,0:T(8,128)(2,1)}, bf16[32,96]{1,0:T(8,128)(2,1)}) custom-call(bf16[32,96]{1,0:T(8,128)(2,1)} %get-tuple-element.10.refs_0_, bf16[256,768]{1,0:T(8,128)(2,1)} %get-tuple-element.11.refs_1_, ...), custom_call_target="tpu_custom_call" | custom-call | tf_op jit(solution)/shard_map/store_results/pallas_call | solution.py:519

commit v6 on v5

--- a/solution.py
+++ b/solution.py
@@ -9,7 +9,7 @@
 F32 = jnp.float32
 BF16 = jnp.bfloat16
 
-NEAR = [(dx, dz) for dz in (2, 1, -1, 0) for dx in (2, 1, 3, 0) if (dx, dz) != (0, 0)]
+NEAR = [(dx, dz) for dz in (0, 1, -1, 2) for dx in (1, 3, 2, 0) if (dx, dz) != (0, 0)]
 FAR = [8, 4, -4]
 GROUP = [(dy, dc) for dy in (2, 1, 3, 0) for dc in (1, 0) if (dy, dc) != (0, 0)]
 N, M, L = len(NEAR), len(GROUP), len(FAR)

time: 80.8 us -> 79.9 us (0.989)
  Pallas kernels: 79.9 us -> 79 us
    pallas_call x1, Pallas kernels: 77.9 us -> 77 us  [shards(): pl.pallas_call(kernel, out_shape=out_shape, in_specs=[hbm] * 5, out_specs...]
where the time goes in v6:
time: 79.9 us; the launch traced here: 79.6 us
  Pallas kernels  79 us (99%)
    pallas_call x1, Pallas kernels, shards(): pl.pallas_call(kernel, out_shape=out_shape, in_specs=[hbm] * 5, out_specs...  77 us
    pallas_call x1, Pallas kernels, shards(): pl.pallas_call(store_kernel, out_shape=out_shape, in_specs=[hbm] * 5, out...  1.98 us

profile of v6, /device:TPU:1, one launch (start us, length us, event | category | flops | bytes accessed | tf_op | source)
XLA Modules:
  0.0 79.6 jit_solution(4097356762527963910)
XLA Ops:
  0.6 77.0 %soft_moe.1 = (bf16[32,96]{1,0:T(8,128)(2,1)}, bf16[256,768]{1,0:T(8,128)(2,1)}, bf16[256,768]{1,0:T(8,128)(2,1)}, bf16[32,96]{1,0:T(8,128)(2,1)}, bf16[32,96]{1,0:T(8,128)(2,1)}) custom-call(bf16[256,768]{1,0:T(8,128)(2,1)} %tok_hbm.1, bf16[32,96]{1,0:T(8,128)(2,1)} %par_hbm.1, bf16[32,96]{1,0:T(8,128)(2,1)} %out_hbm.1, bf16[256,768]{1,0:T(8,128)(2,1)} %go_hbm.1, ...), custom_call_target="tpu_custom_call" | custom-call | flops 1000000000 | bytes 2000000 | tf_op jit(solution)/shard_map/soft_moe/pallas_call | solution.py:463
  77.6 2.0 %store_results.1 = (bf16[32,96]{1,0:T(8,128)(2,1)}, bf16[256,768]{1,0:T(8,128)(2,1)}, bf16[256,768]{1,0:T(8,128)(2,1)}, bf16[32,96]{1,0:T(8,128)(2,1)}, bf16[32,96]{1,0:T(8,128)(2,1)}) custom-call(bf16[32,96]{1,0:T(8,128)(2,1)} %get-tuple-element.10.refs_0_, bf16[256,768]{1,0:T(8,128)(2,1)} %get-tuple-element.11.refs_1_, ...), custom_call_target="tpu_custom_call" | custom-call | tf_op jit(solution)/shard_map/store_results/pallas_call | solution.py:519
